TPU v7x, 256 devices: a whole 4x4x8 slice. The times are simulated.
256 devices in a mesh: lat: 8 (over x_hi, y), lon: 32 (over z, x_lo, core).
Axes of the slice: x: 4 (x_hi: 2, x_lo: 2; x = x_hi * 2 + x_lo), y: 4, z: 8, core: 2. Of those that a mesh axis runs over, the one named last changes fastest.
Arguments:
- fields: bfloat16 [2, 64, 768, 256], P(None, 'lat', 'lon'), may hold values from -6 to 6
- filters: bfloat16 [64, 5, 9, 4], replicated, may hold values from -0.875 to 0.875
- lon_width: int32 [64], replicated, may hold values from 1 to 4, as said below
- disco_weight: bfloat16 [4, 256, 256], replicated, may hold values from -0.1875 to 0.1875
- up_weight: bfloat16 [256, 512], replicated, may hold values from -0.375 to 0.375
- down_weight: bfloat16 [512, 256], replicated, may hold values from -0.25 to 0.25
- cotangent: bfloat16 [2, 64, 768, 256], P(None, 'lat', 'lon'), may hold values from -6 to 6
Outputs:
- output: bfloat16 [2, 64, 768, 256], P(None, 'lat', 'lon')
- back_fields: bfloat16 [2, 64, 768, 256], P(None, 'lat', 'lon')
- grad_disco: float32 [4, 256, 256], replicated
- grad_up: float32 [256, 512], replicated
- grad_down: float32 [512, 256], replicated
Inputs may be any that keep to these rules, and one draw needn't show every extreme that they name: lon_width equals 4 at the 2 rows nearest each pole.
All inputs are finite; a program needn't handle non-finite values.
Results may differ from a plain program's by a relative error of at most 0.013.
Values may be sent and summed in bfloat16 or wider, within the bound.
A program may use at most 128 MiB of HBM per device.

v0:
```python
import jax
import jax.numpy as jnp
from jax import lax
from jax.sharding import PartitionSpec as P

GELU_SCALE = 0.7978845608028654
GELU_CUBE = 0.044715


def with_halo(shard, sides, width, wrap):
    for axis, dim in sides:
        size, length = (lax.axis_size(axis), shard.shape[dim])
        up = [(i, (i + 1) % size) for i in range(size if wrap else size - 1)]
        down = [(j, i) for i, j in up]
        last = lax.slice_in_dim(shard, length - width, length, axis=dim)
        initial = lax.slice_in_dim(shard, 0, width, axis=dim)
        before = lax.ppermute(last, axis, up)
        after = lax.ppermute(initial, axis, down)
        shard = jnp.concatenate([before, shard, after], axis=dim)
    return shard


def gelu_value(pre):
    inner = jnp.tanh(GELU_SCALE * (pre + GELU_CUBE * pre * pre * pre))
    return 0.5 * pre * (1.0 + inner)


def gelu_slope(pre):
    inner = jnp.tanh(GELU_SCALE * (pre + GELU_CUBE * pre * pre * pre))
    return 0.5 * (1.0 + inner) + 0.5 * pre * (1.0 - inner * inner) * GELU_SCALE * (
        1.0 + 3.0 * GELU_CUBE * pre * pre
    )


def masked_filter(filters, lon_width):
    reach_cols = (filters.shape[2] - 1) // 2
    offsets = jnp.abs(jnp.arange(filters.shape[2], dtype=jnp.int32) - reach_cols)
    keep = offsets[None, :] <= lon_width[:, None]
    return jnp.where(keep[:, None, :, None], filters, jnp.zeros_like(filters))


def forward_taps(padded, weights, height, breadth):
    row_taps, col_taps, basis = (weights.shape[1], weights.shape[2], weights.shape[3])
    coeffs = weights.astype(jnp.float32)
    total = jnp.zeros((basis, padded.shape[0], height, breadth, padded.shape[3]), jnp.float32)
    for row_tap in range(row_taps):
        for col_tap in range(col_taps):
            window = padded[:, row_tap : row_tap + height, col_tap : col_tap + breadth].astype(
                jnp.float32
            )
            scale = coeffs[:, row_tap, col_tap, :].T[:, None, :, None, None]
            total = total + window[None] * scale
    return total


def backward_taps(padded, weights, height, breadth):
    row_taps, col_taps = (weights.shape[1], weights.shape[2])
    coeffs = weights.astype(jnp.float32)
    total = jnp.zeros((padded.shape[1], height, breadth, padded.shape[4]), jnp.float32)
    for row_tap in range(row_taps):
        start = row_taps - 1 - row_tap
        for col_tap in range(col_taps):
            first = col_taps - 1 - col_tap
            window = padded[:, :, start : start + height, first : first + breadth].astype(
                jnp.float32
            )
            scale = coeffs[start : start + height, row_tap, col_tap, :].T[:, None, :, None, None]
            total = total + jnp.sum(window * scale, axis=0)
    return total


def per_device(fields, filters, lon_width, disco_weight, up_weight, down_weight, cotangent):
    members, height, breadth, width = fields.shape
    row_taps, col_taps, basis = (filters.shape[1], filters.shape[2], filters.shape[3])
    reach = (row_taps - 1) // 2
    reach_cols = (col_taps - 1) // 2
    weights = masked_filter(filters, lon_width)
    first_row = lax.axis_index("lat") * height
    own_weights = lax.dynamic_slice_in_dim(weights, first_row, height, 0)
    framed = jnp.pad(weights, ((reach, reach), (0, 0), (0, 0), (0, 0)))
    near_weights = lax.dynamic_slice_in_dim(framed, first_row, height + 2 * reach, 0)
    row_ext = with_halo(fields, (("lat", 1),), reach, False)
    padded = with_halo(row_ext, (("lon", 2),), reach_cols, True)
    spread = forward_taps(padded, own_weights, height, breadth).astype(jnp.bfloat16)
    tokens = members * height * breadth
    spread_rows = spread.reshape(basis, tokens, width)
    mixed = jnp.einsum("ktc,kcd->td", spread_rows, disco_weight, preferred_element_type=jnp.float32)
    resid = (fields.reshape(tokens, width).astype(jnp.float32) + mixed).astype(jnp.bfloat16)
    pre = jnp.dot(resid, up_weight, preferred_element_type=jnp.float32)
    hidden = gelu_value(pre).astype(jnp.bfloat16)
    output = (
        resid.astype(jnp.float32) + jnp.dot(hidden, down_weight, preferred_element_type=jnp.float32)
    ).astype(jnp.bfloat16)
    cot = cotangent.reshape(tokens, width)
    back_pre = (
        jnp.dot(cot, down_weight.T, preferred_element_type=jnp.float32) * gelu_slope(pre)
    ).astype(jnp.bfloat16)
    grad_down = jnp.dot(hidden.T, cot, preferred_element_type=jnp.float32)
    grad_up = jnp.dot(resid.T, back_pre, preferred_element_type=jnp.float32)
    back_resid = (
        cot.astype(jnp.float32) + jnp.dot(back_pre, up_weight.T, preferred_element_type=jnp.float32)
    ).astype(jnp.bfloat16)
    grad_disco = jnp.einsum(
        "ktc,td->kcd", spread_rows, back_resid, preferred_element_type=jnp.float32
    )
    back_spread = jnp.einsum(
        "td,kcd->ktc", back_resid, disco_weight, preferred_element_type=jnp.float32
    ).astype(jnp.bfloat16)
    back_spread = back_spread.reshape(basis, members, height, breadth, width)
    back_rows = with_halo(back_spread, (("lat", 2),), reach, False)
    back_padded = with_halo(back_rows, (("lon", 3),), reach_cols, True)
    spread_back = backward_taps(back_padded, near_weights, height, breadth)
    back_fields = (
        back_resid.reshape(members, height, breadth, width).astype(jnp.float32) + spread_back
    ).astype(jnp.bfloat16)
    grad_disco, grad_up, grad_down = lax.psum((grad_disco, grad_up, grad_down), ("lat", "lon"))
    return (
        output.reshape(members, height, breadth, width),
        back_fields,
        grad_disco,
        grad_up,
        grad_down,
    )


def solution(mesh):
    placed = (P(None, "lat", "lon", None), P(), P(), P(), P(), P(), P(None, "lat", "lon", None))
    return jax.shard_map(
        per_device,
        mesh=mesh,
        in_specs=placed,
        out_specs=(P(None, "lat", "lon", None), P(None, "lat", "lon", None), P(), P(), P()),
        check_vma=False,
    )
```

profile of v0, /device:TPU:1, one launch (start us, length us, event | category | flops | bytes accessed | tf_op | source)
XLA Modules:
  0.0 408.8 jit_solution(9934305699909746341)
XLA Ops:
  8.1 1.3 collective-permute-start.1
  9.4 4.7 %collective-permute-start = (bf16[2,2,24,256]{3,2,1,0:T(8,128)(2,1)S(1)}, bf16[2,2,24,256]{3,2,1,0:T(8,128)(2,1)S(1)}, u32[]{:S(2)}, u32[]{:S(2)}) collective-permute-start(bf16[2,2,24,256]{3,2,1,0:T(8,128)(2,1)S(1)} %get-tuple-element.113), channel_id=1, source_target_pairs={{0,32},{32,64},{64,96},{96,128},{128,160},{160,192},{192,224},{1,3... | collective-permute-start | bytes 147464 | tf_op jit(solution)/shard_map/ppermute | solution.py:17
  50.8 2.6 collective-permute-start.2
  55.5 0.9 copy.16
  62.4 1.1 fusion.23
  64.5 1.1 bitcast_convert_fusion.18
  67.4 1.0 bitcast_convert_fusion.11
  68.4 0.9 copy.45
  70.3 0.9 copy.47
  74.1 1.1 fusion.14
  76.2 1.1 bitcast_convert_fusion.36
  78.2 0.9 copy.18
  79.1 1.0 bitcast_convert_fusion.29
  82.0 0.9 copy.28
  84.0 0.9 copy.35
  85.8 1.1 fusion.42
  86.9 0.9 copy.31
  87.9 1.1 bitcast_convert_fusion.22
  89.9 1.0 copy.32
  90.8 1.0 bitcast_convert_fusion.16
  91.8 0.9 copy.40
  93.8 0.9 copy.42
  95.7 1.0 copy.49
  97.6 1.0 fusion.33
  99.6 0.9 copy.14
  101.5 0.9 copy.21
  102.4 0.9 copy.15
  104.4 0.9 copy.22
  105.4 1.1 bitcast_convert_fusion.25
  107.6 10.8 %add_convert_fusion = bf16[4,384,256]{1,2,0:T(8,128)(2,1)S(1)} fusion(f32[4,384]{1,0:T(4,128)} %mul.1715, f32[384,256]{0,1:T(8,128)} %copy.56, f32[4,384]{1,0:T(4,128)} %mul.1708, f32[384,256]{0,1:T(8,128)} %copy.55, f32[4,384]{1,0:T(4,128)} %mul.1701, f32[384,256]{0,1:T(8,128)} %copy.54, f32[4,384]{1,0:T(4,128)} %mul.1694, f32[384,256]{0,1:T(8,128)} %copy.53, ...), kind=kLoop, calls=%fused_computation.85 | loop fusion | flops 35389440 | bytes 18757632 | tf_op jit(solution)/shard_map/convert_element_type | solution.py:84
  119.7 1.2 fusion.54
  121.9 1.1 fusion.61
  123.0 1.4 fusion.51
  124.8 2.3 collective-permute-start.4
  127.1 1.3 collective-permute-start.5
  128.5 1.1 fusion.3
  129.7 3.8 collective-permute-done.5
  133.7 6.3 %collective-permute-start.6 = (bf16[4,2,12,4,256]{4,3,2,1,0:T(4,128)(2,1)S(1)}, bf16[4,2,12,4,256]{4,3,2,1,0:T(4,128)(2,1)S(1)}, u32[]{:S(2)}, u32[]{:S(2)}) collective-permute-start(bf16[4,2,12,4,256]{4,3,2,1,0:T(4,128)(2,1)S(1)} %get-tuple-element.56), channel_id=1, source_target_pairs={{1,0},{2,1},{3,2},{4,3},{5,4},{6,5},{7,6},{8,7},{9,8},{10,9},{11,1... | collective-permute-start | bytes 589832 | tf_op jit(solution)/shard_map/ppermute | solution.py:18
  140.1 1.2 multiply_reduce_fusion.40
  141.8 2.0 collective-permute-done.7
  143.8 1.0 pad_maximum_fusion
  145.0 2.7 multiply_reduce_fusion.43
  147.8 2.6 multiply_reduce_fusion.44
  150.6 2.5 multiply_reduce_fusion.38
  153.2 2.5 multiply_reduce_fusion.39
  156.9 2.0 fusion.12
  158.9 239.0 %all-reduce.4.cloned.1.call-done = (f32[4,256,256]{2,1,0:T(8,128)}, f32[256,512]{1,0:T(8,128)}, f32[512,256]{1,0:T(8,128)}) async-done(((f32[4,256,256]{2,1,0:T(8,128)}, f32[256,512]{1,0:T(8,128)}, f32[512,256]{1,0:T(8,128)}), (f32[4,256,256]{2,1,0:T(8,128)}, f32[256,512]{1,0:T(8,128)}, f32[512,256]{1,0:T(8,128)})) %all-reduce.4.cloned.1.call-update) | async-done | bytes 2097168 | tf_op jit(solution)/shard_map/psum | solution.py:116
  398.0 2.4 copy.66
  (303 shorter events, 72.1 us)
Async XLA Ops:
  7.2 111.3 %copy-start = (bf16[4,256,256]{2,1,0:T(8,128)(2,1)S(1)}, bf16[4,256,256]{2,1,0:T(8,128)(2,1)}, u32[]{:S(2)}) copy-start(bf16[4,256,256]{2,1,0:T(8,128)(2,1)} %param.10) | copy-start | bytes 1572868
  7.2 390.8 %all-reduce.4.cloned.1.call-start = ((), (), s32[]{:S(2)}) async-start(), calls=%async_computation | async-start | bytes 4194304 | tf_op jit(solution)/shard_map/psum | solution.py:116
  8.1 42.6 %collective-permute-start.1 = (bf16[2,2,24,256]{3,2,1,0:T(8,128)(2,1)S(1)}, bf16[2,2,24,256]{3,2,1,0:T(8,128)(2,1)S(1)}, u32[]{:S(2)}, u32[]{:S(2)}) collective-permute-start(bf16[2,2,24,256]{3,2,1,0:T(8,128)(2,1)S(1)} %get-tuple-element.112), channel_id=1, source_target_pairs={{32,0},{64,32},{96,64},{128,96},{160,128},{192,160},{224,192},{33,... | collective-permute-start | bytes 147464 | tf_op jit(solution)/shard_map/ppermute | solution.py:18
  9.4 41.2 %collective-permute-start = (bf16[2,2,24,256]{3,2,1,0:T(8,128)(2,1)S(1)}, bf16[2,2,24,256]{3,2,1,0:T(8,128)(2,1)S(1)}, u32[]{:S(2)}, u32[]{:S(2)}) collective-permute-start(bf16[2,2,24,256]{3,2,1,0:T(8,128)(2,1)S(1)} %get-tuple-element.113), channel_id=1, source_target_pairs={{0,32},{32,64},{64,96},{96,128},{128,160},{160,192},{192,224},{1,3... | collective-permute-start | bytes 147464 | tf_op jit(solution)/shard_map/ppermute | solution.py:17
  20.3 30.3 %copy-start.8 = (bf16[2,8,24,256]{3,2,1,0:T(8,128)(2,1)S(1)}, bf16[2,8,24,256]{3,2,1,0:T(8,128)(2,1)}, u32[]{:S(2)}) copy-start(bf16[2,8,24,256]{3,2,1,0:T(8,128)(2,1)} %param.7) | copy-start | bytes 589828
  50.8 7.5 %collective-permute-start.2 = (bf16[2,12,4,256]{3,2,1,0:T(4,128)(2,1)S(1)}, bf16[2,12,4,256]{3,2,1,0:T(4,128)(2,1)S(1)}, u32[]{:S(2)}, u32[]{:S(2)}) collective-permute-start(bf16[2,12,4,256]{3,2,1,0:T(4,128)(2,1)S(1)} %get-tuple-element.102), channel_id=1, source_target_pairs={{0,1},{1,2},{2,3},{3,4},{4,5},{5,6},{6,7},{7,8},{8,9},{9,10},{10,1... | collective-permute-start | bytes 147464 | tf_op jit(solution)/shard_map/ppermute | solution.py:17
  53.3 5.0 %collective-permute-start.3 = (bf16[2,12,4,256]{3,2,1,0:T(4,128)(2,1)S(1)}, bf16[2,12,4,256]{3,2,1,0:T(4,128)(2,1)S(1)}, u32[]{:S(2)}, u32[]{:S(2)}) collective-permute-start(bf16[2,12,4,256]{3,2,1,0:T(4,128)(2,1)S(1)} %get-tuple-element.103), channel_id=1, source_target_pairs={{1,0},{2,1},{3,2},{4,3},{5,4},{6,5},{7,6},{8,7},{9,8},{10,9},{11,1... | collective-permute-start | bytes 147464 | tf_op jit(solution)/shard_map/ppermute | solution.py:18
  124.8 4.9 %collective-permute-start.4 = (bf16[4,2,2,24,256]{4,3,2,1,0:T(8,128)(2,1)S(1)}, bf16[4,2,2,24,256]{4,3,2,1,0:T(8,128)(2,1)S(1)}, u32[]{:S(2)}, u32[]{:S(2)}) collective-permute-start(bf16[4,2,2,24,256]{4,3,2,1,0:T(8,128)(2,1)S(1)} %get-tuple-element.58), channel_id=1, source_target_pairs={{0,32},{32,64},{64,96},{96,128},{128,160},{160,192},{192,224},{1,3... | collective-permute-start | bytes 589832 | tf_op jit(solution)/shard_map/ppermute | solution.py:17
  127.1 6.4 %collective-permute-start.5 = (bf16[4,2,2,24,256]{4,3,2,1,0:T(8,128)(2,1)S(1)}, bf16[4,2,2,24,256]{4,3,2,1,0:T(8,128)(2,1)S(1)}, u32[]{:S(2)}, u32[]{:S(2)}) collective-permute-start(bf16[4,2,2,24,256]{4,3,2,1,0:T(8,128)(2,1)S(1)} %get-tuple-element.59), channel_id=1, source_target_pairs={{32,0},{64,32},{96,64},{128,96},{160,128},{192,160},{224,192},{33,... | collective-permute-start | bytes 589832 | tf_op jit(solution)/shard_map/ppermute | solution.py:18
  128.5 11.6 %copy-start.57 = (f32[4,8]{1,0:T(4,128)S(1)}, f32[4,8]{1,0:T(4,128)}, u32[]{:S(2)}) copy-start(f32[4,8]{1,0:T(4,128)} %get-tuple-element.156) | copy-start | bytes 388
  128.5 11.6 %copy-start.58 = (f32[4,8]{1,0:T(4,128)S(1)}, f32[4,8]{1,0:T(4,128)}, u32[]{:S(2)}) copy-start(f32[4,8]{1,0:T(4,128)} %get-tuple-element.147) | copy-start | bytes 388
  128.5 11.6 %copy-start.59 = (f32[4,8]{1,0:T(4,128)S(1)}, f32[4,8]{1,0:T(4,128)}, u32[]{:S(2)}) copy-start(f32[4,8]{1,0:T(4,128)} %get-tuple-element.119) | copy-start | bytes 388
  128.5 11.6 %copy-start.60 = (f32[4,8]{1,0:T(4,128)S(1)}, f32[4,8]{1,0:T(4,128)}, u32[]{:S(2)}) copy-start(f32[4,8]{1,0:T(4,128)} %get-tuple-element.128) | copy-start | bytes 388
  133.7 8.1 %collective-permute-start.6 = (bf16[4,2,12,4,256]{4,3,2,1,0:T(4,128)(2,1)S(1)}, bf16[4,2,12,4,256]{4,3,2,1,0:T(4,128)(2,1)S(1)}, u32[]{:S(2)}, u32[]{:S(2)}) collective-permute-start(bf16[4,2,12,4,256]{4,3,2,1,0:T(4,128)(2,1)S(1)} %get-tuple-element.56), channel_id=1, source_target_pairs={{1,0},{2,1},{3,2},{4,3},{5,4},{6,5},{7,6},{8,7},{9,8},{10,9},{11,1... | collective-permute-start | bytes 589832 | tf_op jit(solution)/shard_map/ppermute | solution.py:18
  140.0 3.7 collective-permute-start.7
  141.2 3.5 copy-start.22
  141.3 3.5 copy-start.49
  141.3 3.5 copy-start.50
  141.3 3.5 copy-start.51
  141.3 3.5 copy-start.52
  141.3 3.5 copy-start.53
  141.3 3.5 copy-start.54
  141.3 3.5 copy-start.55
  141.3 3.5 copy-start.56
  144.9 2.8 copy-start.21
  144.9 2.8 copy-start.41
  144.9 2.8 copy-start.42
  144.9 2.8 copy-start.43
  144.9 2.8 copy-start.44
  144.9 2.8 copy-start.45
  144.9 2.8 copy-start.46
  144.9 2.8 copy-start.47
  145.0 2.8 copy-start.48
  147.7 2.7 copy-start.20
  147.7 2.7 copy-start.25
  147.7 2.7 copy-start.26
  147.8 2.7 copy-start.27
  147.8 2.7 copy-start.28
  147.8 2.7 copy-start.29
  147.8 2.7 copy-start.30
  147.8 2.7 copy-start.31
  147.8 2.7 copy-start.32
  150.5 2.6 copy-start.19
  150.5 2.6 copy-start.33
  150.5 2.6 copy-start.34
  150.6 2.6 copy-start.35
  398.0 3.2 copy-start.6
  398.0 4.0 copy-start.1
  (23 other events, 48.0 us)
Sparse Core Ops, SparseCore 0:
  128.6 269.3 all-reduce.3
where the time goes:
time: 410 us; the launch traced here: 409 us
  waiting for transfers between devices  245 us (60%)
  local copies, waits for them, and re-layouts  80.7 us (20%)
  other arithmetic  41.1 us (10%)
  starting transfers between devices  19.4 us (5%)
  between operations  15.4 us (4%)
  matrix products  6.83 us (2%)
    psum x1, waiting for transfers between devices, per_device(): lax.psum((grad_disco, grad_up, grad_down), ('lat', 'lon'))  239 us
    mul x134, local copies, waits for them, and re-layouts, forward_taps(): total = total + window[None] * scale  71.5 us
    reduce_sum x7, other arithmetic, backward_taps(): total = total + jnp.sum(window * scale, axis=0)  12.3 us
    convert_element_type x1, other arithmetic, per_device(): forward_taps(padded, own_weights, height, breadth).astype(jnp.bfloat16)  10.8 us
    ppermute x4, starting transfers between devices, with_halo(): after = lax.ppermute(initial, axis, down)  9.82 us
    ppermute x4, starting transfers between devices, with_halo(): before = lax.ppermute(last, axis, up)  9.51 us
    mul x24, other arithmetic, forward_taps(): total = total + window[None] * scale  8.4 us
  transfers between devices with their start and end apart: 9, of which 5 were waited for; matrix products, arithmetic and copies ran while one was open for 14% of the time, Pallas kernels for 0%

commit v1 on v0

v1 whole, which is shorter than its diff:
```python
import functools

import jax
import jax.numpy as jnp
import numpy as np
from jax import lax
from jax.experimental import pallas as pl
from jax.experimental.pallas import tpu as pltpu
from jax.sharding import PartitionSpec as P

GELU_SCALE = 0.7978845608028654
GELU_CUBE = 0.044715
MESH = pl.DeviceIdType.MESH
F32 = jnp.float32
BF16 = jnp.bfloat16

M, ROWS, CELLS, C, FF, K = 2, 8, 24, 256, 512, 4
NLAT = 64
A_TAPS, B_TAPS = 5, 9
PAIRS = ROWS // 2
TOK = M * ROWS * CELLS
BLOCK = 80
NK = 3 * BLOCK


def constants():
    sel_f = np.zeros((256, K * 256), np.float32)
    sel_b = np.zeros((256, K * 256), np.float32)
    for a in range(A_TAPS):
        for b in range(B_TAPS):
            for k in range(K):
                s = a * B_TAPS * K + b * K + k
                sel_f[s, k * 256 + a * 32 + b] = 1
                sel_b[s, k * 256 + (4 - a) * 32 + 8 - b] = 1
    perm = np.zeros((2, 256, 256), np.float32)
    for i2 in range(2):
        for a in range(A_TAPS):
            p, r2 = divmod(i2 + a, 2)
            for jj in range(32):
                if jj < 4:
                    col = p * BLOCK + 48 + r2 * 4 + jj
                elif jj < 28:
                    col = p * BLOCK + r2 * CELLS + jj - 4
                else:
                    col = p * BLOCK + 64 + r2 * 4 + jj - 28
                perm[i2, a * 32 + jj, col] = 1
    edge = np.zeros((2 * PAIRS * 16, ROWS * CELLS), np.float32)
    for side in range(2):
        for q in range(PAIRS):
            for r2 in range(2):
                for j in range(4):
                    cell = (CELLS - 4 + j) if side == 0 else j
                    edge[(side * PAIRS + q) * 16 + r2 * 4 + j, (q * 2 + r2) * CELLS + cell] = 1
    return [x.astype(jnp.bfloat16) for x in (sel_f, sel_b, perm, edge)]


def dot(a, b, dims=((1,), (0,))):
    return lax.dot_general(a, b, (dims, ((), ())), preferred_element_type=F32)


def kernel(
    lw, fields, cot, disco, up, down, filt, sel_f, sel_b, perm, edge,
    out_o, out_b, out_g,
    x, y, stage, vcot, vdisco, vup, vdown, vfilt, vself, vselb, vperm, vedge,
    vline, lines, band, tap_f, tap_b, spread, pre, cd, hidden, bpre, resid, bres, vout, vback,
    g, rc, a1, r1, a2, r2, rz, o,
    lsem, osem, hs, hr, cs, cr, s1s, s1r, s2s, s2r, zs, zr, g2s, g2r, g1s, g1r, gcs, gcr,
):
    lat, lon = lax.axis_index("lat"), lax.axis_index("lon")
    x_hi, yy = lat // 4, lat % 4
    zz, x_lo, core = lon // 4, (lon // 2) % 2, lon % 2
    xx = x_hi * 2 + x_lo

    def at_x(d):
        v = (xx + d) % 4
        return ((v // 2) * 4 + yy, zz * 4 + (v % 2) * 2 + core)

    def at_y(d):
        return (x_hi * 4 + (yy + d) % 4, lon)

    def at_z(d):
        return (lat, ((zz + d) % 8) * 4 + x_lo * 2 + core)

    pair = (lat, zz * 4 + x_lo * 2 + (1 - core))
    right, left = (lon + 1) % 32, (lon + 31) % 32
    has_up, has_down = lat > 0, lat < 7

    loads = [
        pltpu.make_async_copy(fields, x.at[:, 1:5, 0:48], lsem.at[0]),
        pltpu.make_async_copy(edge, vedge, lsem.at[1]),
        pltpu.make_async_copy(filt, vfilt, lsem.at[2]),
        pltpu.make_async_copy(sel_f, vself, lsem.at[3]),
        pltpu.make_async_copy(perm, vperm, lsem.at[4]),
        pltpu.make_async_copy(cot, vcot, lsem.at[5]),
        pltpu.make_async_copy(down, vdown, lsem.at[6]),
        pltpu.make_async_copy(disco, vdisco, lsem.at[7]),
        pltpu.make_async_copy(up, vup, lsem.at[8]),
        pltpu.make_async_copy(sel_b, vselb, lsem.at[9]),
    ]
    for c in loads:
        c.start()

    barrier = pltpu.get_barrier_semaphore()

    def hello(dev):
        pl.semaphore_signal(barrier, inc=1, device_id=dev, device_id_type=MESH)

    hello((lat, right))
    hello((lat, left))

    @pl.when(has_up)
    def _():
        for v in (left, lon, right):
            hello((lat - 1, v))

    @pl.when(has_down)
    def _():
        for v in (left, lon, right):
            hello((lat + 1, v))

    hello(pair)
    for d in range(1, 4):
        hello(at_x(d))
        hello(at_y(d))
    for d in range(1, 8):
        hello(at_z(d))

    zero48 = jnp.zeros((M, BLOCK, C), BF16)

    @pl.when(lat == 0)
    def _():
        x[:, 0] = zero48
        y[:, 0] = zero48

    @pl.when(lat == 7)
    def _():
        x[:, 5] = zero48
        y[:, 5] = zero48

    def rdma(src, dst, ss, rs, dev):
        return pltpu.make_async_remote_copy(
            src_ref=src, dst_ref=dst, send_sem=ss, recv_sem=rs, device_id=dev, device_id_type=MESH
        )

    def halo(buf, ph):
        st = stage.at[ph]

        def lon_copies():
            return [
                rdma(st.at[0], buf.at[:, 1:5, 48:64], hs.at[ph, 0], hr.at[ph, 0], (lat, right)),
                rdma(st.at[1], buf.at[:, 1:5, 64:80], hs.at[ph, 1], hr.at[ph, 1], (lat, left)),
            ]

        def to_down():
            return [
                rdma(buf.at[:, 4, 0:48], buf.at[:, 0, 0:48], hs.at[ph, 2], hr.at[ph, 2], (lat + 1, lon)),
                rdma(st.at[0, :, 3], buf.at[:, 0, 48:64], hs.at[ph, 3], hr.at[ph, 3], (lat + 1, right)),
                rdma(st.at[1, :, 3], buf.at[:, 0, 64:80], hs.at[ph, 4], hr.at[ph, 4], (lat + 1, left)),
            ]

        def to_up():
            return [
                rdma(buf.at[:, 1, 0:48], buf.at[:, 5, 0:48], hs.at[ph, 5], hr.at[ph, 5], (lat - 1, lon)),
                rdma(st.at[0, :, 0], buf.at[:, 5, 48:64], hs.at[ph, 6], hr.at[ph, 6], (lat - 1, right)),
                rdma(st.at[1, :, 0], buf.at[:, 5, 64:80], hs.at[ph, 7], hr.at[ph, 7], (lat - 1, left)),
            ]

        def start():
            @pl.when(has_down)
            def _():
                for c in to_down():
                    c.start()

            @pl.when(has_up)
            def _():
                for c in to_up():
                    c.start()

            for c in lon_copies():
                c.start()

        def recv():
            for c in lon_copies():
                c.wait_recv()

            @pl.when(has_up)
            def _():
                for c in to_down():
                    c.wait_recv()

            @pl.when(has_down)
            def _():
                for c in to_up():
                    c.wait_recv()

        def sent():
            for c in lon_copies():
                c.wait_send()

            @pl.when(has_down)
            def _():
                for c in to_down():
                    c.wait_send()

            @pl.when(has_up)
            def _():
                for c in to_up():
                    c.wait_send()

        return start, recv, sent

    halo_x = halo(x, 0)
    halo_y = halo(y, 1)

    def own(buf, m):
        return buf[m, 1:5, 0:48].reshape(ROWS * CELLS, C)

    def fill_stage(buf, ph):
        for m in range(M):
            e = dot(vedge[...], own(buf, m)).astype(BF16).reshape(2, PAIRS, 16, C)
            stage[ph, 0, m] = e[0]
            stage[ph, 1, m] = e[1]

    loads[0].wait()
    loads[1].wait()
    fill_stage(x, 0)
    pl.semaphore_wait(
        barrier, 16 + 3 * has_up.astype(jnp.int32) + 3 * has_down.astype(jnp.int32)
    )
    halo_x[0]()

    loads[2].wait()
    first = lat * ROWS - 2
    row_sel = (
        lax.broadcasted_iota(jnp.int32, (16, NLAT), 1)
        == lax.broadcasted_iota(jnp.int32, (16, NLAT), 0) + first
    )
    near = dot(jnp.where(row_sel, 1.0, 0.0).astype(BF16), vfilt[...]).astype(BF16)
    line_row = lax.broadcasted_iota(jnp.int32, (16, K * 256), 0)
    reach = jnp.zeros((16, K * 256), jnp.int32)
    for r in range(12):
        reach = jnp.where(line_row == r, lw[jnp.clip(first + r, 0, NLAT - 1)], reach)
    lane = lax.broadcasted_iota(jnp.int32, (16, K * 256), 1)
    keep = jnp.abs((lane & 31) - 4) <= reach

    def bands(get_line, tap):
        for i in range(ROWS):
            q, i2 = divmod(i, 2)
            parts = []
            for k in range(K):
                line = jnp.broadcast_to(get_line(i, k), (CELLS, 256))
                parts.append(
                    jnp.concatenate(
                        [
                            pltpu.roll(line[:, h * 128 : (h + 1) * 128], 0, 1, stride=1, stride_axis=0)
                            for h in range(2)
                        ],
                        axis=1,
                    )
                )
            band[i2, q * 96 : (q + 1) * 96] = jnp.concatenate(parts, axis=0).astype(BF16)
        res = [dot(band[i2], vperm[i2]) for i2 in range(2)]
        for q in range(PAIRS):
            for k in range(K):
                at = q * 96 + k * CELLS
                both = jnp.concatenate([res[0][at : at + CELLS], res[1][at : at + CELLS]], axis=0)
                tap[q, k * 48 : (k + 1) * 48] = both.astype(BF16)

    loads[3].wait()
    loads[4].wait()
    vline[...] = jnp.where(keep, dot(near, vself[...]), 0.0)
    bands(lambda i, k: vline[i + 2 : i + 3, k * 256 : (k + 1) * 256], tap_f)

    loads[5].wait()
    loads[6].wait()
    cd[...] = dot(vcot[...], vdown[...], ((1,), (1,)))
    loads[7].wait()
    loads[8].wait()
    loads[9].wait()

    def stencil(tap, buf, dst):
        for q in range(PAIRS):
            for m in range(M):
                res = dot(tap[q][:, :NK], buf[m, q : q + 3].reshape(NK, C)).astype(BF16)
                for k in range(K):
                    at = m * 192 + q * 48
                    dst[at : at + 48, k * C : (k + 1) * C] = res[k * 48 : (k + 1) * 48]

    halo_x[1]()
    stencil(tap_f, x, spread)

    for m in range(M):
        mixed = dot(spread[m * 192 : (m + 1) * 192], vdisco[...])
        resid[m * 192 : (m + 1) * 192] = (own(x, m).astype(F32) + mixed).astype(BF16)
    pre[...] = dot(resid[...], vup[...])

    @pl.loop(0, TOK // 16)
    def _(n):
        at = pl.ds(pl.multiple_of(n * 16, 16), 16)
        p = pre[at]
        pp = p * p
        t = jnp.tanh(GELU_SCALE * p * (1.0 + GELU_CUBE * pp))
        h = 0.5 * (1.0 + t)
        hidden[at] = (p * h).astype(BF16)
        slope = h + 0.5 * p * (1.0 - t * t) * GELU_SCALE * (1.0 + 3.0 * GELU_CUBE * pp)
        bpre[at] = (cd[at] * slope).astype(BF16)

    rows0 = ((0,), (0,))

    def put(n, value):
        g[n] = value.astype(BF16).reshape(2, 4, 4, 16, C)

    def core_copy(n):
        return rdma(g.at[n, 1 - core], rc.at[n], cs.at[n], cr.at[n], pair)

    put(0, dot(hidden[...], vcot[...], rows0))
    core_copy(0).start()
    gu = dot(resid[...], bpre[...], rows0)
    put(1, jnp.concatenate([gu[:, :C], gu[:, C:]], axis=0))
    core_copy(1).start()

    br = (vcot[...].astype(F32) + dot(bpre[...], vup[...], ((1,), (1,)))).astype(BF16)
    bres[...] = br
    for m in range(M):
        y[m, 1:5, 0:48] = br[m * 192 : (m + 1) * 192].reshape(PAIRS, 48, C)
    fill_stage(y, 1)
    halo_y[0]()
    for n in range(2):
        put(2 + n, dot(spread[:, n * 512 : (n + 1) * 512], bres[...], rows0))
        core_copy(2 + n).start()

    def ways(n):
        return ((at_x, xx), (at_y, yy)) if n % 2 == 0 else ((at_y, yy), (at_x, xx))

    def s1_copies(n):
        peer, me = ways(n)[0]
        return [
            rdma(a1.at[n, (me + d) % 4], r1.at[n, d - 1], s1s.at[n, d - 1], s1r.at[n, d - 1], peer(d))
            for d in range(1, 4)
        ]

    def s2_copies(n):
        peer, me = ways(n)[1]
        return [
            rdma(a2.at[n, (me + d) % 4], r2.at[n, d - 1], s2s.at[n, d - 1], s2r.at[n, d - 1], peer(d))
            for d in range(1, 4)
        ]

    def z_copies(h):
        return [
            rdma(rz.at[h, zz], rz.at[h, zz], zs.at[h, d - 1], zr.at[h, d - 1], at_z(d))
            for d in range(1, 8)
        ]

    def g2_copies(n):
        (_, m1), (peer, m2) = ways(n)
        ref = o.at[n, core, m1, m2]
        return [rdma(ref, ref, g2s.at[n, d - 1], g2r.at[n, d - 1], peer(d)) for d in range(1, 4)]

    def g1_copies(n):
        peer, m1 = ways(n)[0]
        ref = o.at[n, core, m1]
        return [rdma(ref, ref, g1s.at[n, d - 1], g1r.at[n, d - 1], peer(d)) for d in range(1, 4)]

    def gc_copy(n):
        ref = o.at[n, core]
        return rdma(ref, ref, gcs.at[n], gcr.at[n], pair)

    def start(cs_):
        for c in cs_:
            c.start()

    def recv(cs_):
        for c in cs_:
            c.wait_recv()

    def do_core(n):
        core_copy(n).wait_recv()
        a1[n] = (g[n, core].astype(F32) + rc[n].astype(F32)).astype(BF16)
        start(s1_copies(n))

    def do_s1(n):
        recv(s1_copies(n))
        me = ways(n)[0][1]
        v = a1[n, me].astype(F32)
        for d in range(3):
            v = v + r1[n, d].astype(F32)
        a2[n] = v.astype(BF16)
        start(s2_copies(n))

    def do_s2(h):
        for e in range(2):
            n = 2 * h + e
            recv(s2_copies(n))
            me = ways(n)[1][1]
            v = a2[n, me].astype(F32)
            for d in range(3):
                v = v + r2[n, d].astype(F32)
            rz[h, zz, e] = v.astype(BF16)
        start(z_copies(h))

    def do_z(h):
        recv(z_copies(h))
        v = rz[h, 0].astype(F32)
        for d in range(1, 8):
            v = v + rz[h, d].astype(F32)
        v = v.astype(BF16)
        for e in range(2):
            n = 2 * h + e
            (_, m1), (_, m2) = ways(n)
            o[n, core, m1, m2] = v[e]
            start(g2_copies(n))

    def do_g2(n):
        recv(g2_copies(n))
        start(g1_copies(n))

    def do_g1(n):
        recv(g1_copies(n))
        gc_copy(n).start()

    do_core(0)
    do_core(1)
    do_core(2)
    do_core(3)

    vline[...] = jnp.where(keep, dot(near, vselb[...]), 0.0)
    group = (lax.broadcasted_iota(jnp.int32, (8, K * 256), 1) // 32) % 8
    total = jnp.zeros((8, K * 256), F32)
    for r in range(A_TAPS):
        total = total + jnp.where(group == r, vline[r : r + 8], 0.0)
    lines[...] = total
    bands(lambda i, k: lines[i : i + 1, k * 256 : (k + 1) * 256], tap_b)

    for n in range(4):
        do_s1(n)
    vout[...] = (resid[...].astype(F32) + dot(hidden[...], vdown[...])).astype(BF16)
    put_o = pltpu.make_async_copy(vout, out_o, osem.at[0])
    put_o.start()
    do_s2(0)
    do_s2(1)

    halo_y[1]()
    stencil(tap_b, y, spread)
    do_z(0)
    do_z(1)
    for m in range(M):
        at = slice(m * 192, (m + 1) * 192)
        acc = bres[at].astype(F32)
        for k in range(K):
            acc = acc + dot(
                spread[at, k * C : (k + 1) * C], vdisco[k * C : (k + 1) * C], ((1,), (1,))
            )
        vback[at] = acc.astype(BF16)
    put_b = pltpu.make_async_copy(vback, out_b, osem.at[1])
    put_b.start()
    for n in range(4):
        do_g2(n)
    for n in range(4):
        do_g1(n)
    for n in range(4):
        gc_copy(n).wait_recv()
    put_g = pltpu.make_async_copy(o, out_g, osem.at[2])
    put_g.start()

    halo_x[2]()
    halo_y[2]()
    for n in range(4):
        core_copy(n).wait_send()
        for c in s1_copies(n) + s2_copies(n) + g2_copies(n) + g1_copies(n):
            c.wait_send()
        gc_copy(n).wait_send()
    for h in range(2):
        for c in z_copies(h):
            c.wait_send()
    put_o.wait()
    put_b.wait()
    put_g.wait()


def per_device(fields, filters, lon_width, disco_weight, up_weight, down_weight, cotangent):
    flat = jnp.pad(filters.reshape(NLAT, A_TAPS * B_TAPS * K), ((0, 0), (0, 76)))
    sel_f, sel_b, perm, edge = [jnp.asarray(v) for v in constants()]
    anyspec = pl.BlockSpec(memory_space=pl.ANY)
    dma = pltpu.SemaphoreType.DMA
    vm = pltpu.VMEM
    scratch = [
        vm((M, 6, BLOCK, C), BF16),
        vm((M, 6, BLOCK, C), BF16),
        vm((2, 2, M, PAIRS, 16, C), BF16),
        vm((TOK, C), BF16),
        vm((K * C, C), BF16),
        vm((C, FF), BF16),
        vm((FF, C), BF16),
        vm((NLAT, 256), BF16),
        vm((256, K * 256), BF16),
        vm((256, K * 256), BF16),
        vm((2, 256, 256), BF16),
        vm((2 * PAIRS * 16, ROWS * CELLS), BF16),
        vm((16, K * 256), F32),
        vm((8, K * 256), F32),
        vm((2, PAIRS * 96, 256), BF16),
        vm((PAIRS, 192, 256), BF16),
        vm((PAIRS, 192, 256), BF16),
        vm((TOK, K * C), BF16),
        vm((TOK, FF), F32),
        vm((TOK, FF), F32),
        vm((TOK, FF), BF16),
        vm((TOK, FF), BF16),
        vm((TOK, C), BF16),
        vm((TOK, C), BF16),
        vm((TOK, C), BF16),
        vm((TOK, C), BF16),
        vm((4, 2, 4, 4, 16, C), BF16),
        vm((4, 4, 4, 16, C), BF16),
        vm((4, 4, 4, 16, C), BF16),
        vm((4, 3, 4, 16, C), BF16),
        vm((4, 4, 16, C), BF16),
        vm((4, 3, 16, C), BF16),
        vm((2, 8, 2, 16, C), BF16),
        vm((4, 2, 4, 4, 16, C), BF16),
        dma((10,)),
        dma((3,)),
        dma((2, 8)),
        dma((2, 8)),
        dma((4,)),
        dma((4,)),
        dma((4, 3)),
        dma((4, 3)),
        dma((4, 3)),
        dma((4, 3)),
        dma((2, 7)),
        dma((2, 7)),
        dma((4, 3)),
        dma((4, 3)),
        dma((4, 3)),
        dma((4, 3)),
        dma((4,)),
        dma((4,)),
    ]
    out_o, out_b, out_g = pl.pallas_call(
        kernel,
        out_shape=(
            jax.ShapeDtypeStruct((TOK, C), BF16),
            jax.ShapeDtypeStruct((TOK, C), BF16),
            jax.ShapeDtypeStruct((4, 2, 4, 4, 16, C), BF16),
        ),
        in_specs=[pl.BlockSpec(memory_space=pltpu.SMEM)] + [anyspec] * 10,
        out_specs=(anyspec, anyspec, anyspec),
        scratch_shapes=scratch,
        compiler_params=pltpu.CompilerParams(
            collective_id=0, has_side_effects=True, vmem_limit_bytes=40 * 2**20
        ),
    )(
        lon_width,
        fields.reshape(M, PAIRS, 48, C),
        cotangent.reshape(TOK, C),
        disco_weight.reshape(K * C, C),
        up_weight,
        down_weight,
        flat,
        sel_f,
        sel_b,
        perm,
        edge,
    )
    grads = out_g.reshape(4, 512, C).astype(F32)
    grad_up = jnp.concatenate([grads[1, :C], grads[1, C:]], axis=1)
    shape = fields.shape
    return (
        out_o.reshape(shape),
        out_b.reshape(shape),
        grads[2:].reshape(K, C, C),
        grad_up,
        grads[0],
    )


def solution(mesh):
    placed = (P(None, "lat", "lon", None), P(), P(), P(), P(), P(), P(None, "lat", "lon", None))
    return jax.shard_map(
        per_device,
        mesh=mesh,
        in_specs=placed,
        out_specs=(P(None, "lat", "lon", None), P(None, "lat", "lon", None), P(), P(), P()),
        check_vma=False,
    )
```

time: 410 us -> 66 us (0.16)
  waiting for transfers between devices: 245 us -> 0 us
  local copies, waits for them, and re-layouts: 80.7 us -> 13.6 us
  Pallas kernels: 0 us -> 50.2 us
  other arithmetic: 41.1 us -> 1.12 us
  starting transfers between devices: 19.4 us -> 0 us
  between operations: 15.4 us -> 0.69 us
  matrix products: 6.83 us -> 0 us
    psum x1 -> x0, waiting for transfers between devices: 239 us -> none  [per_device(): lax.psum((grad_disco, grad_up, grad_down), ('lat', 'lon'))]
    mul x136 -> x0, local copies, waits for them, and re-layouts: 72.3 us -> none  [the longest x134 71.5 us: forward_taps(): total = total + window[None] * scale]
    pallas_call x0 -> x1, Pallas kernels: none -> 50.2 us  [per_device(): pl.pallas_call(kernel, out_shape=(jax.ShapeDtypeStruct((TOK, C), BF16), j...]
    ppermute x8 -> x0, starting transfers between devices: 19.3 us -> none  [the longest x4 9.82 us: with_halo(): after = lax.ppermute(initial, axis, down)]
    convert_element_type x4 -> x1, other arithmetic: 13.1 us -> 0.27 us  [per_device(): grads = out_g.reshape(4, 512, C).astype(F32)]
    reduce_sum x7 -> x0, other arithmetic: 12.3 us -> none  [backward_taps(): total = total + jnp.sum(window * scale, axis=0)]
    mul x24 -> x0, other arithmetic: 8.4 us -> none  [forward_taps(): total = total + window[None] * scale]
    dot_general x9 -> x0, matrix products: 6.83 us -> none  [the longest x1 1.4 us: per_device(): jnp.einsum('ktc,td->kcd', spread_rows, back_resid, preferred_element_type...]
  transfers between devices with their start and end apart: 9 -> 0, of which waited for: 5 -> 0; matrix products, arithmetic and copies ran while one was open for 14% -> 0% of each run, Pallas kernels for 0% -> 0%
where the time goes in v1:
time: 66 us; the launch traced here: 65.6 us
  Pallas kernels  50.2 us (76%)
  local copies, waits for them, and re-layouts  13.6 us (21%)
  other arithmetic  1.12 us (2%)
  between operations  0.69 us (1%)
    pallas_call x1, Pallas kernels, per_device(): pl.pallas_call(kernel, out_shape=(jax.ShapeDtypeStruct((TOK, C), BF16), j...  50.2 us
    unnamed x22, local copies, waits for them, and re-layouts  10.7 us

profile of v1, /device:TPU:1, one launch (start us, length us, event | category | flops | bytes accessed | tf_op | source)
XLA Modules:
  0.0 65.6 jit_solution(8452353770563391772)
XLA Ops:
  0.6 0.8 %reshape.40 = bf16[64,180]{0,1:T(8,128)(2,1)S(1)} reshape(bf16[64,5,9,4]{0,3,2,1:T(4,128)(2,1)} %param.12) | data formatting | bytes 46080 | tf_op jit(solution)/shard_map/reshape | solution.py:482
  1.5 0.1 copy.17
  1.6 0.0 copy-start
  1.6 1.0 %copy-done = bf16[4,256,256]{2,1,0:T(8,128)(2,1)S(1)} copy-done((bf16[4,256,256]{2,1,0:T(8,128)(2,1)S(1)}, bf16[4,256,256]{2,1,0:T(8,128)(2,1)}, u32[]{:S(2)}) %copy-start) | copy-done | bytes 524312
  2.6 0.0 copy-start.1
  2.6 1.0 %copy-done.1 = bf16[256,1024]{1,0:T(8,128)(2,1)S(1)} copy-done((bf16[256,1024]{1,0:T(8,128)(2,1)S(1)}, bf16[256,1024]{1,0:T(8,128)(2,1)}, u32[]{:S(2)}) %copy-start.1) | copy-done | bytes 524312
  3.7 0.0 copy-start.2
  3.7 1.0 %copy-done.2 = bf16[256,1024]{1,0:T(8,128)(2,1)S(1)} copy-done((bf16[256,1024]{1,0:T(8,128)(2,1)S(1)}, bf16[256,1024]{1,0:T(8,128)(2,1)}, u32[]{:S(2)}) %copy-start.2) | copy-done | bytes 524312
  4.7 0.0 copy-start.3
  4.7 0.9 %copy-done.3 = bf16[256,512]{1,0:T(8,128)(2,1)S(1)} copy-done((bf16[256,512]{1,0:T(8,128)(2,1)S(1)}, bf16[256,512]{1,0:T(8,128)(2,1)}, u32[]{:S(2)}) %copy-start.3) | copy-done | bytes 262168
  5.6 0.0 copy-start.4
  5.7 0.9 %copy-done.4 = bf16[512,256]{1,0:T(8,128)(2,1)S(1)} copy-done((bf16[512,256]{1,0:T(8,128)(2,1)S(1)}, bf16[512,256]{1,0:T(8,128)(2,1)}, u32[]{:S(2)}) %copy-start.4) | copy-done | bytes 262168
  6.6 0.0 copy-start.5
  6.6 0.9 %copy-done.5 = bf16[2,256,256]{2,1,0:T(8,128)(2,1)S(1)} copy-done((bf16[2,256,256]{2,1,0:T(8,128)(2,1)S(1)}, bf16[2,256,256]{2,1,0:T(8,128)(2,1)}, u32[]{:S(2)}) %copy-start.5) | copy-done | bytes 262168
  7.5 0.0 copy-start.6
  7.6 0.9 %copy-done.6 = bf16[2,8,24,256]{3,2,1,0:T(8,128)(2,1)S(1)} copy-done((bf16[2,8,24,256]{3,2,1,0:T(8,128)(2,1)S(1)}, bf16[2,8,24,256]{3,2,1,0:T(8,128)(2,1)}, u32[]{:S(2)}) %copy-start.6) | copy-done | bytes 196632
  8.5 0.0 copy-start.7
  8.5 0.9 %copy-done.7 = bf16[2,8,24,256]{3,2,1,0:T(8,128)(2,1)S(1)} copy-done((bf16[2,8,24,256]{3,2,1,0:T(8,128)(2,1)S(1)}, bf16[2,8,24,256]{3,2,1,0:T(8,128)(2,1)}, u32[]{:S(2)}) %copy-start.7) | copy-done | bytes 196632
  9.4 0.0 copy-start.8
  9.4 0.8 %copy-done.8 = bf16[128,192]{1,0:T(8,128)(2,1)S(1)} copy-done((bf16[128,192]{1,0:T(8,128)(2,1)S(1)}, bf16[128,192]{1,0:T(8,128)(2,1)}, u32[]{:S(2)}) %copy-start.8) | copy-done | bytes 49176
  10.2 0.0 copy-start.9
  10.2 0.7 copy-done.9
  10.9 50.2 %shard_map.146 = (bf16[384,256]{1,0:T(8,128)(2,1)S(1)}, bf16[384,256]{1,0:T(8,128)(2,1)S(1)}, bf16[4,2,4,4,16,256]{5,4,3,2,1,0:T(8,128)(2,1)S(1)}) custom-call(s32[64]{0:T(128)S(1)} %copy-done.9, bf16[2,4,48,256]{3,2,1,0:T(8,128)(2,1)S(1)} %bitcast.15, bf16[384,256]{1,0:T(8,128)(2,1)S(1)} %bitcast.16, bf16[1024,256]{1,0:T(8,128)(2,1)S(1)} %bitcast.14, ...), custom_call_target="tpu_custom_call" | custom-call | tf_op jit(solution)/shard_map/pallas_call | solution.py:541
  61.1 0.3 convert_element_type.8
  61.4 0.9 %pad_maximum_fusion = f32[256,512]{1,0:T(8,128)} fusion(f32[256,256]{1,0:T(8,128)S(1)} %get-tuple-element.12, f32[256,256]{1,0:T(8,128)S(1)} %get-tuple-element.11), kind=kLoop, calls=%fused_computation | loop fusion | flops 131072 | bytes 1048576 | tf_op jit(solution)/shard_map/concatenate | solution.py:568
  62.2 1.1 %slice.18 = f32[2,2,4,4,16,256]{5,4,3,2,1,0:T(8,128)} slice(bf16[4,2,4,4,16,256]{5,4,3,2,1,0:T(8,128)(2,1)S(1)} %get-tuple-element.10), slice={[2:4], [0:2], [0:4], [0:4], [0:16], [0:256]} | slice | bytes 2097152 | tf_op jit(solution)/shard_map/slice | solution.py:573
  63.4 0.8 %slice.21 = f32[1,2,4,4,16,256]{5,4,3,2,1,0:T(8,128)} slice(bf16[4,2,4,4,16,256]{5,4,3,2,1,0:T(8,128)(2,1)S(1)} %get-tuple-element.10), slice={[0:1], [0:2], [0:4], [0:4], [0:16], [0:256]} | slice | bytes 1048576 | tf_op jit(solution)/shard_map/slice | solution.py:575
  64.2 0.7 %copy.20 = bf16[2,8,24,256]{3,2,1,0:T(8,128)(2,1)} copy(bf16[2,8,24,256]{3,2,1,0:T(8,128)(2,1)S(1)} %bitcast.18) | data formatting | bytes 393216
  64.9 0.7 %copy.21 = bf16[2,8,24,256]{3,2,1,0:T(8,128)(2,1)} copy(bf16[2,8,24,256]{3,2,1,0:T(8,128)(2,1)S(1)} %bitcast.17) | data formatting | bytes 393216
  (2 shorter events, 0.0 us)
Async XLA Ops:
  1.6 1.0 %copy-start = (bf16[4,256,256]{2,1,0:T(8,128)(2,1)S(1)}, bf16[4,256,256]{2,1,0:T(8,128)(2,1)}, u32[]{:S(2)}) copy-start(bf16[4,256,256]{2,1,0:T(8,128)(2,1)} %param.14) | copy-start | bytes 1572868
  2.6 1.0 %copy-start.1 = (bf16[256,1024]{1,0:T(8,128)(2,1)S(1)}, bf16[256,1024]{1,0:T(8,128)(2,1)}, u32[]{:S(2)}) copy-start(bf16[256,1024]{1,0:T(8,128)(2,1)} %constant.11.clone.sel_f) | copy-start | bytes 1572868
  3.7 1.0 %copy-start.2 = (bf16[256,1024]{1,0:T(8,128)(2,1)S(1)}, bf16[256,1024]{1,0:T(8,128)(2,1)}, u32[]{:S(2)}) copy-start(bf16[256,1024]{1,0:T(8,128)(2,1)} %constant.12.clone.sel_b) | copy-start | bytes 1572868
  4.7 0.9 %copy-start.3 = (bf16[256,512]{1,0:T(8,128)(2,1)S(1)}, bf16[256,512]{1,0:T(8,128)(2,1)}, u32[]{:S(2)}) copy-start(bf16[256,512]{1,0:T(8,128)(2,1)} %up.1) | copy-start | bytes 786436
  5.6 0.9 %copy-start.4 = (bf16[512,256]{1,0:T(8,128)(2,1)S(1)}, bf16[512,256]{1,0:T(8,128)(2,1)}, u32[]{:S(2)}) copy-start(bf16[512,256]{1,0:T(8,128)(2,1)} %down.1) | copy-start | bytes 786436
  6.6 0.9 %copy-start.5 = (bf16[2,256,256]{2,1,0:T(8,128)(2,1)S(1)}, bf16[2,256,256]{2,1,0:T(8,128)(2,1)}, u32[]{:S(2)}) copy-start(bf16[2,256,256]{2,1,0:T(8,128)(2,1)} %constant.13.clone.perm) | copy-start | bytes 786436
  7.5 0.9 %copy-start.6 = (bf16[2,8,24,256]{3,2,1,0:T(8,128)(2,1)S(1)}, bf16[2,8,24,256]{3,2,1,0:T(8,128)(2,1)}, u32[]{:S(2)}) copy-start(bf16[2,8,24,256]{3,2,1,0:T(8,128)(2,1)} %param.11) | copy-start | bytes 589828
  8.5 0.9 %copy-start.7 = (bf16[2,8,24,256]{3,2,1,0:T(8,128)(2,1)S(1)}, bf16[2,8,24,256]{3,2,1,0:T(8,128)(2,1)}, u32[]{:S(2)}) copy-start(bf16[2,8,24,256]{3,2,1,0:T(8,128)(2,1)} %param.17) | copy-start | bytes 589828
  9.4 0.8 %copy-start.8 = (bf16[128,192]{1,0:T(8,128)(2,1)S(1)}, bf16[128,192]{1,0:T(8,128)(2,1)}, u32[]{:S(2)}) copy-start(bf16[128,192]{1,0:T(8,128)(2,1)} %constant.14.clone.edge) | copy-start | bytes 147460
  10.2 0.7 copy-start.9

commit v2 on v1

--- a/solution.py
+++ b/solution.py
@@ -21,15 +21,16 @@
 TOK = M * ROWS * CELLS
 BLOCK = 80
 NK = 3 * BLOCK
+NF = A_TAPS * B_TAPS * 8
 
 
 def constants():
-    sel_f = np.zeros((256, K * 256), np.float32)
-    sel_b = np.zeros((256, K * 256), np.float32)
+    sel_f = np.zeros((NF, K * 256), np.float32)
+    sel_b = np.zeros((NF, K * 256), np.float32)
     for a in range(A_TAPS):
         for b in range(B_TAPS):
             for k in range(K):
-                s = a * B_TAPS * K + b * K + k
+                s = (a * B_TAPS + b) * 8 + k
                 sel_f[s, k * 256 + a * 32 + b] = 1
                 sel_b[s, k * 256 + (4 - a) * 32 + 8 - b] = 1
     perm = np.zeros((2, 256, 256), np.float32)
@@ -60,11 +61,11 @@
 
 def kernel(
     lw, fields, cot, disco, up, down, filt, sel_f, sel_b, perm, edge,
-    out_o, out_b, out_g,
-    x, y, stage, vcot, vdisco, vup, vdown, vfilt, vself, vselb, vperm, vedge,
-    vline, lines, band, tap_f, tap_b, spread, pre, cd, hidden, bpre, resid, bres, vout, vback,
-    g, rc, a1, r1, a2, r2, rz, o,
-    lsem, osem, hs, hr, cs, cr, s1s, s1r, s2s, s2r, zs, zr, g2s, g2r, g1s, g1r, gcs, gcr,
+    vout, vback, o,
+    x, y, stage, vcot, vdisco, vup, vdown, vfilt, filt8, vself, vselb, vperm, vedge,
+    vline, lines, band, tap_f, tap_b, spread, pre, cd, hidden, bpre, resid, bres,
+    g, rc, a1, r1, a2, r2, rz,
+    lsem, hs, hr, cs, cr, s1s, s1r, s2s, s2r, zs, zr, g2s, g2r, g1s, g1r, gcs, gcr,
 ):
     lat, lon = lax.axis_index("lat"), lax.axis_index("lon")
     x_hi, yy = lat // 4, lat % 4
@@ -230,12 +231,15 @@
     halo_x[0]()
 
     loads[2].wait()
+    filt8[...] = jnp.zeros_like(filt8)
+    for n in range(A_TAPS * B_TAPS):
+        filt8[n * 8 : n * 8 + K] = vfilt[n].astype(F32)
     first = lat * ROWS - 2
     row_sel = (
         lax.broadcasted_iota(jnp.int32, (16, NLAT), 1)
         == lax.broadcasted_iota(jnp.int32, (16, NLAT), 0) + first
     )
-    near = dot(jnp.where(row_sel, 1.0, 0.0).astype(BF16), vfilt[...]).astype(BF16)
+    near = dot(jnp.where(row_sel, 1.0, 0.0).astype(BF16), filt8[...].astype(BF16), ((1,), (1,))).astype(BF16)
     line_row = lax.broadcasted_iota(jnp.int32, (16, K * 256), 0)
     reach = jnp.zeros((16, K * 256), jnp.int32)
     for r in range(12):
@@ -274,9 +278,17 @@
     loads[5].wait()
     loads[6].wait()
     cd[...] = dot(vcot[...], vdown[...], ((1,), (1,)))
+    loads[9].wait()
+    vline[...] = jnp.where(keep, dot(near, vselb[...]), 0.0)
+    group = (lax.broadcasted_iota(jnp.int32, (8, K * 256), 1) // 32) % 8
+    total = jnp.zeros((8, K * 256), F32)
+    for r in range(A_TAPS):
+        total = total + jnp.where(group == r, vline[r : r + 8], 0.0)
+    lines[...] = total
+    bands(lambda i, k: lines[i : i + 1, k * 256 : (k + 1) * 256], tap_b)
+
     loads[7].wait()
     loads[8].wait()
-    loads[9].wait()
 
     def stencil(tap, buf, dst):
         for q in range(PAIRS):
@@ -318,16 +330,6 @@
     gu = dot(resid[...], bpre[...], rows0)
     put(1, jnp.concatenate([gu[:, :C], gu[:, C:]], axis=0))
     core_copy(1).start()
-
-    br = (vcot[...].astype(F32) + dot(bpre[...], vup[...], ((1,), (1,)))).astype(BF16)
-    bres[...] = br
-    for m in range(M):
-        y[m, 1:5, 0:48] = br[m * 192 : (m + 1) * 192].reshape(PAIRS, 48, C)
-    fill_stage(y, 1)
-    halo_y[0]()
-    for n in range(2):
-        put(2 + n, dot(spread[:, n * 512 : (n + 1) * 512], bres[...], rows0))
-        core_copy(2 + n).start()
 
     def ways(n):
         return ((at_x, xx), (at_y, yy)) if n % 2 == 0 else ((at_y, yy), (at_x, xx))
@@ -419,31 +421,30 @@
         recv(g1_copies(n))
         gc_copy(n).start()
 
+    br = (vcot[...].astype(F32) + dot(bpre[...], vup[...], ((1,), (1,)))).astype(BF16)
+    bres[...] = br
+    for m in range(M):
+        y[m, 1:5, 0:48] = br[m * 192 : (m + 1) * 192].reshape(PAIRS, 48, C)
+    fill_stage(y, 1)
     do_core(0)
     do_core(1)
+    for n in range(2):
+        put(2 + n, dot(spread[:, n * 512 : (n + 1) * 512], bres[...], rows0))
+        core_copy(2 + n).start()
+
     do_core(2)
     do_core(3)
-
-    vline[...] = jnp.where(keep, dot(near, vselb[...]), 0.0)
-    group = (lax.broadcasted_iota(jnp.int32, (8, K * 256), 1) // 32) % 8
-    total = jnp.zeros((8, K * 256), F32)
-    for r in range(A_TAPS):
-        total = total + jnp.where(group == r, vline[r : r + 8], 0.0)
-    lines[...] = total
-    bands(lambda i, k: lines[i : i + 1, k * 256 : (k + 1) * 256], tap_b)
-
     for n in range(4):
         do_s1(n)
-    vout[...] = (resid[...].astype(F32) + dot(hidden[...], vdown[...])).astype(BF16)
-    put_o = pltpu.make_async_copy(vout, out_o, osem.at[0])
-    put_o.start()
     do_s2(0)
     do_s2(1)
 
+    halo_y[0]()
+    vout[...] = (resid[...].astype(F32) + dot(hidden[...], vdown[...])).astype(BF16)
+    do_z(0)
+    do_z(1)
     halo_y[1]()
     stencil(tap_b, y, spread)
-    do_z(0)
-    do_z(1)
     for m in range(M):
         at = slice(m * 192, (m + 1) * 192)
         acc = bres[at].astype(F32)
@@ -452,16 +453,14 @@
                 spread[at, k * C : (k + 1) * C], vdisco[k * C : (k + 1) * C], ((1,), (1,))
             )
         vback[at] = acc.astype(BF16)
-    put_b = pltpu.make_async_copy(vback, out_b, osem.at[1])
-    put_b.start()
+
     for n in range(4):
         do_g2(n)
     for n in range(4):
         do_g1(n)
+
     for n in range(4):
         gc_copy(n).wait_recv()
-    put_g = pltpu.make_async_copy(o, out_g, osem.at[2])
-    put_g.start()
 
     halo_x[2]()
     halo_y[2]()
@@ -473,14 +472,33 @@
     for h in range(2):
         for c in z_copies(h):
             c.wait_send()
-    put_o.wait()
-    put_b.wait()
-    put_g.wait()
+
+
+def finish(o, b, g, out_o, out_b, out_disco, out_up, out_down, wdisco, wup, wdown, sem):
+    copies = [
+        pltpu.make_async_copy(o, out_o, sem.at[0]),
+        pltpu.make_async_copy(b, out_b, sem.at[1]),
+        pltpu.make_async_copy(wdisco, out_disco, sem.at[2]),
+        pltpu.make_async_copy(wdown, out_down, sem.at[3]),
+        pltpu.make_async_copy(wup, out_up, sem.at[4]),
+    ]
+    copies[0].start()
+    copies[1].start()
+    wdisco[...] = g[2:].reshape(K * C, C).astype(F32)
+    copies[2].start()
+    wdown[...] = g[0].reshape(FF, C).astype(F32)
+    copies[3].start()
+    wup[:, :C] = g[1, 0].reshape(C, C).astype(F32)
+    wup[:, C:] = g[1, 1].reshape(C, C).astype(F32)
+    copies[4].start()
+    for c in copies:
+        c.wait()
 
 
 def per_device(fields, filters, lon_width, disco_weight, up_weight, down_weight, cotangent):
-    flat = jnp.pad(filters.reshape(NLAT, A_TAPS * B_TAPS * K), ((0, 0), (0, 76)))
+    flat = filters.transpose(1, 2, 3, 0).reshape(A_TAPS * B_TAPS, K, NLAT)
     sel_f, sel_b, perm, edge = [jnp.asarray(v) for v in constants()]
+    vspec = pl.BlockSpec(memory_space=pltpu.VMEM)
     anyspec = pl.BlockSpec(memory_space=pl.ANY)
     dma = pltpu.SemaphoreType.DMA
     vm = pltpu.VMEM
@@ -492,9 +510,10 @@
         vm((K * C, C), BF16),
         vm((C, FF), BF16),
         vm((FF, C), BF16),
-        vm((NLAT, 256), BF16),
-        vm((256, K * 256), BF16),
-        vm((256, K * 256), BF16),
+        vm((A_TAPS * B_TAPS, K, NLAT), BF16),
+        vm((NF, NLAT), F32),
+        vm((NF, K * 256), BF16),
+        vm((NF, K * 256), BF16),
         vm((2, 256, 256), BF16),
         vm((2 * PAIRS * 16, ROWS * CELLS), BF16),
         vm((16, K * 256), F32),
@@ -509,8 +528,6 @@
         vm((TOK, FF), BF16),
         vm((TOK, C), BF16),
         vm((TOK, C), BF16),
-        vm((TOK, C), BF16),
-        vm((TOK, C), BF16),
         vm((4, 2, 4, 4, 16, C), BF16),
         vm((4, 4, 4, 16, C), BF16),
         vm((4, 4, 4, 16, C), BF16),
@@ -518,9 +535,7 @@
         vm((4, 4, 16, C), BF16),
         vm((4, 3, 16, C), BF16),
         vm((2, 8, 2, 16, C), BF16),
-        vm((4, 2, 4, 4, 16, C), BF16),
         dma((10,)),
-        dma((3,)),
         dma((2, 8)),
         dma((2, 8)),
         dma((4,)),
@@ -538,18 +553,18 @@
         dma((4,)),
         dma((4,)),
     ]
-    out_o, out_b, out_g = pl.pallas_call(
+    inner = pl.pallas_call(
         kernel,
         out_shape=(
-            jax.ShapeDtypeStruct((TOK, C), BF16),
-            jax.ShapeDtypeStruct((TOK, C), BF16),
-            jax.ShapeDtypeStruct((4, 2, 4, 4, 16, C), BF16),
+            vm((TOK, C), BF16),
+            vm((TOK, C), BF16),
+            vm((4, 2, 4, 4, 16, C), BF16),
         ),
-        in_specs=[pl.BlockSpec(memory_space=pltpu.SMEM)] + [anyspec] * 10,
-        out_specs=(anyspec, anyspec, anyspec),
+        in_specs=[pl.BlockSpec(memory_space=pltpu.SMEM)] + [pl.BlockSpec(memory_space=pltpu.HBM)] * 10,
+        out_specs=[vspec] * 3,
         scratch_shapes=scratch,
         compiler_params=pltpu.CompilerParams(
-            collective_id=0, has_side_effects=True, vmem_limit_bytes=40 * 2**20
+            collective_id=0, has_side_effects=True, vmem_limit_bytes=62 * 2**20
         ),
     )(
         lon_width,
@@ -564,16 +579,22 @@
         perm,
         edge,
     )
-    grads = out_g.reshape(4, 512, C).astype(F32)
-    grad_up = jnp.concatenate([grads[1, :C], grads[1, C:]], axis=1)
+    out, back, disco, up, down = pl.pallas_call(
+        finish,
+        out_shape=(
+            jax.ShapeDtypeStruct((TOK, C), BF16),
+            jax.ShapeDtypeStruct((TOK, C), BF16),
+            jax.ShapeDtypeStruct((K * C, C), F32),
+            jax.ShapeDtypeStruct((C, FF), F32),
+            jax.ShapeDtypeStruct((FF, C), F32),
+        ),
+        in_specs=[vspec] * 3,
+        out_specs=[pl.BlockSpec(memory_space=pltpu.HBM)] * 5,
+        scratch_shapes=[vm((K * C, C), F32), vm((C, FF), F32), vm((FF, C), F32), dma((5,))],
+        compiler_params=pltpu.CompilerParams(vmem_limit_bytes=16 * 2**20),
+    )(*[pltpu.with_memory_space_constraint(v, pltpu.VMEM) for v in inner])
     shape = fields.shape
-    return (
-        out_o.reshape(shape),
-        out_b.reshape(shape),
-        grads[2:].reshape(K, C, C),
-        grad_up,
-        grads[0],
-    )
+    return out.reshape(shape), back.reshape(shape), disco.reshape(K, C, C), up, down
 
 
 def solution(mesh):

time: 66 us -> 50.2 us (0.76)
  local copies, waits for them, and re-layouts: 13.6 us -> 0 us
  other arithmetic: 1.12 us -> 0 us
  Pallas kernels: 50.2 us -> 49.5 us
    unnamed x22 -> x0, local copies, waits for them, and re-layouts: 10.7 us -> none
    slice x2 -> x0, local copies, waits for them, and re-layouts: 1.95 us -> none  [the longest x1 1.1 us: per_device(): grads[2:].reshape(K, C, C)]
    reshape x2 -> x0, local copies, waits for them, and re-layouts: 0.91 us -> none  [per_device(): filters.reshape(NLAT, A_TAPS * B_TAPS * K)]
    concatenate x1 -> x0, other arithmetic: 0.85 us -> none  [per_device(): grad_up = jnp.concatenate([grads[1, :C], grads[1, C:]], axis=1)]
    pallas_call x1 -> x2, Pallas kernels: 50.2 us -> 49.5 us  [the longest x1 48 us: per_device(): pl.pallas_call(kernel, out_shape=(vm((TOK, C), BF16), vm((TOK, C), BF16),...]
where the time goes in v2:
time: 50.2 us; the launch traced here: 50.1 us
  Pallas kernels  49.5 us (99%)
  between operations  0.64 us (1%)
    pallas_call x1, Pallas kernels, per_device(): pl.pallas_call(kernel, out_shape=(vm((TOK, C), BF16), vm((TOK, C), BF16),...  48 us
    pallas_call x1, Pallas kernels, per_device(): pl.pallas_call(finish, out_shape=(jax.ShapeDtypeStruct((TOK, C), BF16), j...  1.49 us

profile of v2, /device:TPU:1, one launch (start us, length us, event | category | flops | bytes accessed | tf_op | source)
XLA Modules:
  0.0 50.1 jit_solution(4666776582626933303)
XLA Ops:
  0.6 48.0 %shard_map.146 = (bf16[384,256]{1,0:T(8,128)(2,1)S(1)}, bf16[384,256]{1,0:T(8,128)(2,1)S(1)}, bf16[4,2,4,4,16,256]{5,4,3,2,1,0:T(8,128)(2,1)S(1)}) custom-call(s32[64]{0:T(128)} %lw.1, bf16[2,4,48,256]{3,2,1,0:T(8,128)(2,1)} %bitcast.10, bf16[384,256]{1,0:T(8,128)(2,1)} %bitcast.11, bf16[1024,256]{1,0:T(8,128)(2,1)} %bitcast.9, bf16[256,512]{1,0:T(8,128)(2,1)} %up.1, ...), custom_call_target="tpu_custom_call" | custom-call | tf_op jit(solution)/shard_map/pallas_call | solution.py:556
  48.6 1.5 %shard_map.147 = (bf16[384,256]{1,0:T(8,128)(2,1)}, bf16[384,256]{1,0:T(8,128)(2,1)}, f32[1024,256]{1,0:T(8,128)}, f32[256,512]{1,0:T(8,128)}, f32[512,256]{1,0:T(8,128)}) custom-call(bf16[384,256]{1,0:T(8,128)(2,1)S(1)} %get-tuple-element.13.o, bf16[384,256]{1,0:T(8,128)(2,1)S(1)} %get-tuple-element.14.b, ...), custom_call_target="tpu_custom_call" | custom-call | tf_op jit(solution)/shard_map/pallas_call | solution.py:582

commit v3 on v2

--- a/solution.py
+++ b/solution.py
@@ -22,6 +22,11 @@
 BLOCK = 80
 NK = 3 * BLOCK
 NF = A_TAPS * B_TAPS * 8
+PLANE = sorted(
+    [(dx, dy) for dx in range(4) for dy in range(4) if dx or dy],
+    key=lambda t: (-min(t[0], 4 - t[0]) - min(t[1], 4 - t[1]), t),
+)
+RING = (4, 3, 5, 2, 6, 1, 7)
 
 
 def constants():
@@ -64,20 +69,17 @@
     vout, vback, o,
     x, y, stage, vcot, vdisco, vup, vdown, vfilt, filt8, vself, vselb, vperm, vedge,
     vline, lines, band, tap_f, tap_b, spread, pre, cd, hidden, bpre, resid, bres,
-    g, rc, a1, r1, a2, r2, rz,
-    lsem, hs, hr, cs, cr, s1s, s1r, s2s, s2r, zs, zr, g2s, g2r, g1s, g1r, gcs, gcr,
+    g, rc, a1, r1, rz,
+    lsem, hs, hr, cs, cr, s1s, s1r, zs, zr, g1s, g1r, gcs, gcr,
 ):
     lat, lon = lax.axis_index("lat"), lax.axis_index("lon")
     x_hi, yy = lat // 4, lat % 4
     zz, x_lo, core = lon // 4, (lon // 2) % 2, lon % 2
     xx = x_hi * 2 + x_lo
 
-    def at_x(d):
-        v = (xx + d) % 4
-        return ((v // 2) * 4 + yy, zz * 4 + (v % 2) * 2 + core)
-
-    def at_y(d):
-        return (x_hi * 4 + (yy + d) % 4, lon)
+    def at_xy(dx, dy):
+        v = (xx + dx) % 4
+        return ((v // 2) * 4 + (yy + dy) % 4, zz * 4 + (v % 2) * 2 + core)
 
     def at_z(d):
         return (lat, ((zz + d) % 8) * 4 + x_lo * 2 + core)
@@ -120,10 +122,9 @@
             hello((lat + 1, v))
 
     hello(pair)
-    for d in range(1, 4):
-        hello(at_x(d))
-        hello(at_y(d))
-    for d in range(1, 8):
+    for dx, dy in PLANE:
+        hello(at_xy(dx, dy))
+    for d in RING:
         hello(at_z(d))
 
     zero48 = jnp.zeros((M, BLOCK, C), BF16)
@@ -226,7 +227,7 @@
     loads[1].wait()
     fill_stage(x, 0)
     pl.semaphore_wait(
-        barrier, 16 + 3 * has_up.astype(jnp.int32) + 3 * has_down.astype(jnp.int32)
+        barrier, 25 + 3 * has_up.astype(jnp.int32) + 3 * has_down.astype(jnp.int32)
     )
     halo_x[0]()
 
@@ -331,94 +332,61 @@
     put(1, jnp.concatenate([gu[:, :C], gu[:, C:]], axis=0))
     core_copy(1).start()
 
-    def ways(n):
-        return ((at_x, xx), (at_y, yy)) if n % 2 == 0 else ((at_y, yy), (at_x, xx))
-
-    def s1_copies(n):
-        peer, me = ways(n)[0]
+    def plane_copies(n):
         return [
-            rdma(a1.at[n, (me + d) % 4], r1.at[n, d - 1], s1s.at[n, d - 1], s1r.at[n, d - 1], peer(d))
-            for d in range(1, 4)
+            rdma(
+                a1.at[n, (xx + dx) % 4, (yy + dy) % 4], r1.at[n, i], s1s.at[n, i], s1r.at[n, i],
+                at_xy(dx, dy),
+            )
+            for i, (dx, dy) in enumerate(PLANE)
         ]
 
-    def s2_copies(n):
-        peer, me = ways(n)[1]
+    def z_copies(n):
+        ref = rz.at[n, zz]
+        return [rdma(ref, ref, zs.at[n, i], zr.at[n, i], at_z(d)) for i, d in enumerate(RING)]
+
+    def gather_copies(n):
+        ref = o.at[n, core, xx, yy]
         return [
-            rdma(a2.at[n, (me + d) % 4], r2.at[n, d - 1], s2s.at[n, d - 1], s2r.at[n, d - 1], peer(d))
-            for d in range(1, 4)
+            rdma(ref, ref, g1s.at[n, i], g1r.at[n, i], at_xy(dx, dy))
+            for i, (dx, dy) in enumerate(PLANE)
         ]
-
-    def z_copies(h):
-        return [
-            rdma(rz.at[h, zz], rz.at[h, zz], zs.at[h, d - 1], zr.at[h, d - 1], at_z(d))
-            for d in range(1, 8)
-        ]
-
-    def g2_copies(n):
-        (_, m1), (peer, m2) = ways(n)
-        ref = o.at[n, core, m1, m2]
-        return [rdma(ref, ref, g2s.at[n, d - 1], g2r.at[n, d - 1], peer(d)) for d in range(1, 4)]
-
-    def g1_copies(n):
-        peer, m1 = ways(n)[0]
-        ref = o.at[n, core, m1]
-        return [rdma(ref, ref, g1s.at[n, d - 1], g1r.at[n, d - 1], peer(d)) for d in range(1, 4)]
 
     def gc_copy(n):
         ref = o.at[n, core]
         return rdma(ref, ref, gcs.at[n], gcr.at[n], pair)
 
-    def start(cs_):
-        for c in cs_:
+    def start(copies):
+        for c in copies:
             c.start()
 
-    def recv(cs_):
-        for c in cs_:
+    def recv(copies):
+        for c in copies:
             c.wait_recv()
 
     def do_core(n):
         core_copy(n).wait_recv()
         a1[n] = (g[n, core].astype(F32) + rc[n].astype(F32)).astype(BF16)
-        start(s1_copies(n))
-
-    def do_s1(n):
-        recv(s1_copies(n))
-        me = ways(n)[0][1]
-        v = a1[n, me].astype(F32)
-        for d in range(3):
+        start(plane_copies(n))
+
+    def do_plane(n):
+        recv(plane_copies(n))
+        v = a1[n, xx, yy].astype(F32)
+        for d in range(15):
             v = v + r1[n, d].astype(F32)
-        a2[n] = v.astype(BF16)
-        start(s2_copies(n))
-
-    def do_s2(h):
-        for e in range(2):
-            n = 2 * h + e
-            recv(s2_copies(n))
-            me = ways(n)[1][1]
-            v = a2[n, me].astype(F32)
-            for d in range(3):
-                v = v + r2[n, d].astype(F32)
-            rz[h, zz, e] = v.astype(BF16)
-        start(z_copies(h))
-
-    def do_z(h):
-        recv(z_copies(h))
-        v = rz[h, 0].astype(F32)
+        rz[n, zz] = v.astype(BF16)
+        start(z_copies(n))
+
+    def do_z(n):
+        recv(z_copies(n))
+        v = rz[n, 0].astype(F32)
         for d in range(1, 8):
-            v = v + rz[h, d].astype(F32)
-        v = v.astype(BF16)
-        for e in range(2):
-            n = 2 * h + e
-            (_, m1), (_, m2) = ways(n)
-            o[n, core, m1, m2] = v[e]
-            start(g2_copies(n))
-
-    def do_g2(n):
-        recv(g2_copies(n))
-        start(g1_copies(n))
-
-    def do_g1(n):
-        recv(g1_copies(n))
+            v = v + rz[n, d].astype(F32)
+        o[n, core, xx, yy] = v.astype(BF16)
+        start(gather_copies(n))
+
+    def do_gather(n):
+        recv(gather_copies(n))
         gc_copy(n).start()
 
     br = (vcot[...].astype(F32) + dot(bpre[...], vup[...], ((1,), (1,)))).astype(BF16)
@@ -434,15 +402,13 @@
 
     do_core(2)
     do_core(3)
+    halo_y[0]()
     for n in range(4):
-        do_s1(n)
-    do_s2(0)
-    do_s2(1)
-
-    halo_y[0]()
+        do_plane(n)
+
     vout[...] = (resid[...].astype(F32) + dot(hidden[...], vdown[...])).astype(BF16)
-    do_z(0)
-    do_z(1)
+    for n in range(4):
+        do_z(n)
     halo_y[1]()
     stencil(tap_b, y, spread)
     for m in range(M):
@@ -455,9 +421,7 @@
         vback[at] = acc.astype(BF16)
 
     for n in range(4):
-        do_g2(n)
-    for n in range(4):
-        do_g1(n)
+        do_gather(n)
 
     for n in range(4):
         gc_copy(n).wait_recv()
@@ -466,12 +430,9 @@
     halo_y[2]()
     for n in range(4):
         core_copy(n).wait_send()
-        for c in s1_copies(n) + s2_copies(n) + g2_copies(n) + g1_copies(n):
+        for c in plane_copies(n) + z_copies(n) + gather_copies(n):
             c.wait_send()
         gc_copy(n).wait_send()
-    for h in range(2):
-        for c in z_copies(h):
-            c.wait_send()
 
 
 def finish(o, b, g, out_o, out_b, out_disco, out_up, out_down, wdisco, wup, wdown, sem):
@@ -531,25 +492,19 @@
         vm((4, 2, 4, 4, 16, C), BF16),
         vm((4, 4, 4, 16, C), BF16),
         vm((4, 4, 4, 16, C), BF16),
-        vm((4, 3, 4, 16, C), BF16),
-        vm((4, 4, 16, C), BF16),
-        vm((4, 3, 16, C), BF16),
-        vm((2, 8, 2, 16, C), BF16),
+        vm((4, 15, 16, C), BF16),
+        vm((4, 8, 16, C), BF16),
         dma((10,)),
         dma((2, 8)),
         dma((2, 8)),
         dma((4,)),
         dma((4,)),
-        dma((4, 3)),
-        dma((4, 3)),
-        dma((4, 3)),
-        dma((4, 3)),
-        dma((2, 7)),
-        dma((2, 7)),
-        dma((4, 3)),
-        dma((4, 3)),
-        dma((4, 3)),
-        dma((4, 3)),
+        dma((4, 15)),
+        dma((4, 15)),
+        dma((4, 7)),
+        dma((4, 7)),
+        dma((4, 15)),
+        dma((4, 15)),
         dma((4,)),
         dma((4,)),
     ]

time: 50.2 us -> 46.6 us (0.928)
  Pallas kernels: 49.5 us -> 45.9 us
    pallas_call x1, Pallas kernels: 48 us -> 44.4 us  [per_device(): pl.pallas_call(kernel, out_shape=(vm((TOK, C), BF16), vm((TOK, C), BF16),...]
where the time goes in v3:
time: 46.6 us; the launch traced here: 46.5 us
  Pallas kernels  45.9 us (98%)
  between operations  0.64 us (1%)
    pallas_call x1, Pallas kernels, per_device(): pl.pallas_call(kernel, out_shape=(vm((TOK, C), BF16), vm((TOK, C), BF16),...  44.4 us
    pallas_call x1, Pallas kernels, per_device(): pl.pallas_call(finish, out_shape=(jax.ShapeDtypeStruct((TOK, C), BF16), j...  1.49 us

profile of v3, /device:TPU:1, one launch (start us, length us, event | category | flops | bytes accessed | tf_op | source)
XLA Modules:
  0.0 46.5 jit_solution(2268983067608510328)
XLA Ops:
  0.6 44.4 %shard_map.146 = (bf16[384,256]{1,0:T(8,128)(2,1)S(1)}, bf16[384,256]{1,0:T(8,128)(2,1)S(1)}, bf16[4,2,4,4,16,256]{5,4,3,2,1,0:T(8,128)(2,1)S(1)}) custom-call(s32[64]{0:T(128)} %lw.1, bf16[2,4,48,256]{3,2,1,0:T(8,128)(2,1)} %bitcast.10, bf16[384,256]{1,0:T(8,128)(2,1)} %bitcast.11, bf16[1024,256]{1,0:T(8,128)(2,1)} %bitcast.9, bf16[256,512]{1,0:T(8,128)(2,1)} %up.1, ...), custom_call_target="tpu_custom_call" | custom-call | tf_op jit(solution)/shard_map/pallas_call | solution.py:511
  45.1 1.5 %shard_map.147 = (bf16[384,256]{1,0:T(8,128)(2,1)}, bf16[384,256]{1,0:T(8,128)(2,1)}, f32[1024,256]{1,0:T(8,128)}, f32[256,512]{1,0:T(8,128)}, f32[512,256]{1,0:T(8,128)}) custom-call(bf16[384,256]{1,0:T(8,128)(2,1)S(1)} %get-tuple-element.13.o, bf16[384,256]{1,0:T(8,128)(2,1)S(1)} %get-tuple-element.14.b, ...), custom_call_target="tpu_custom_call" | custom-call | tf_op jit(solution)/shard_map/pallas_call | solution.py:537

commit v4 on v3

--- a/solution.py
+++ b/solution.py
@@ -66,10 +66,10 @@
 
 def kernel(
     lw, fields, cot, disco, up, down, filt, sel_f, sel_b, perm, edge,
-    vout, vback, o,
+    vout, vback, disco_out, up_out, down_out,
     x, y, stage, vcot, vdisco, vup, vdown, vfilt, filt8, vself, vselb, vperm, vedge,
     vline, lines, band, tap_f, tap_b, spread, pre, cd, hidden, bpre, resid, bres,
-    g, rc, a1, r1, rz,
+    g, rc, a1, r1, rz, o,
     lsem, hs, hr, cs, cr, s1s, s1r, zs, zr, g1s, g1r, gcs, gcr,
 ):
     lat, lon = lax.axis_index("lat"), lax.axis_index("lon")
@@ -280,14 +280,6 @@
     loads[6].wait()
     cd[...] = dot(vcot[...], vdown[...], ((1,), (1,)))
     loads[9].wait()
-    vline[...] = jnp.where(keep, dot(near, vselb[...]), 0.0)
-    group = (lax.broadcasted_iota(jnp.int32, (8, K * 256), 1) // 32) % 8
-    total = jnp.zeros((8, K * 256), F32)
-    for r in range(A_TAPS):
-        total = total + jnp.where(group == r, vline[r : r + 8], 0.0)
-    lines[...] = total
-    bands(lambda i, k: lines[i : i + 1, k * 256 : (k + 1) * 256], tap_b)
-
     loads[7].wait()
     loads[8].wait()
 
@@ -335,7 +327,7 @@
     def plane_copies(n):
         return [
             rdma(
-                a1.at[n, (xx + dx) % 4, (yy + dy) % 4], r1.at[n, i], s1s.at[n, i], s1r.at[n, i],
+                a1.at[n, (xx + dx) % 4, (yy + dy) % 4], r1.at[n, i], s1s.at[n], s1r.at[n],
                 at_xy(dx, dy),
             )
             for i, (dx, dy) in enumerate(PLANE)
@@ -343,13 +335,13 @@
 
     def z_copies(n):
         ref = rz.at[n, zz]
-        return [rdma(ref, ref, zs.at[n, i], zr.at[n, i], at_z(d)) for i, d in enumerate(RING)]
+        return [rdma(ref, ref, zs.at[n], zr.at[n], at_z(d)) for d in RING]
 
     def gather_copies(n):
         ref = o.at[n, core, xx, yy]
         return [
-            rdma(ref, ref, g1s.at[n, i], g1r.at[n, i], at_xy(dx, dy))
-            for i, (dx, dy) in enumerate(PLANE)
+            rdma(ref, ref, g1s.at[n], g1r.at[n], at_xy(dx, dy))
+            for dx, dy in PLANE
         ]
 
     def gc_copy(n):
@@ -360,9 +352,9 @@
         for c in copies:
             c.start()
 
-    def recv(copies):
-        for c in copies:
-            c.wait_recv()
+    def wait_all(blocks, sem):
+        ref = r1.at[0, 0:blocks]
+        pltpu.make_async_copy(ref, ref, sem).wait()
 
     def do_core(n):
         core_copy(n).wait_recv()
@@ -370,7 +362,7 @@
         start(plane_copies(n))
 
     def do_plane(n):
-        recv(plane_copies(n))
+        wait_all(15, s1r.at[n])
         v = a1[n, xx, yy].astype(F32)
         for d in range(15):
             v = v + r1[n, d].astype(F32)
@@ -378,7 +370,7 @@
         start(z_copies(n))
 
     def do_z(n):
-        recv(z_copies(n))
+        wait_all(7, zr.at[n])
         v = rz[n, 0].astype(F32)
         for d in range(1, 8):
             v = v + rz[n, d].astype(F32)
@@ -386,7 +378,7 @@
         start(gather_copies(n))
 
     def do_gather(n):
-        recv(gather_copies(n))
+        wait_all(15, g1r.at[n])
         gc_copy(n).start()
 
     br = (vcot[...].astype(F32) + dot(bpre[...], vup[...], ((1,), (1,)))).astype(BF16)
@@ -403,12 +395,27 @@
     do_core(2)
     do_core(3)
     halo_y[0]()
+    vline[...] = jnp.where(keep, dot(near, vselb[...]), 0.0)
+    group = (lax.broadcasted_iota(jnp.int32, (8, K * 256), 1) // 32) % 8
+    total = jnp.zeros((8, K * 256), F32)
+    for r in range(A_TAPS):
+        total = total + jnp.where(group == r, vline[r : r + 8], 0.0)
+    lines[...] = total
+    bands(lambda i, k: lines[i : i + 1, k * 256 : (k + 1) * 256], tap_b)
+
     for n in range(4):
         do_plane(n)
 
     vout[...] = (resid[...].astype(F32) + dot(hidden[...], vdown[...])).astype(BF16)
+    halo_x[2]()
+    halo_y[2]()
+    for n in range(4):
+        core_copy(n).wait_send()
+        wait_all(15, s1s.at[n])
     for n in range(4):
         do_z(n)
+    for n in range(4):
+        wait_all(7, zs.at[n])
     halo_y[1]()
     stencil(tap_b, y, spread)
     for m in range(M):
@@ -424,34 +431,26 @@
         do_gather(n)
 
     for n in range(4):
+        wait_all(15, g1s.at[n])
+    for n in range(4):
         gc_copy(n).wait_recv()
-
-    halo_x[2]()
-    halo_y[2]()
-    for n in range(4):
-        core_copy(n).wait_send()
-        for c in plane_copies(n) + z_copies(n) + gather_copies(n):
-            c.wait_send()
+        whole = o[n].astype(F32)
+        if n == 0:
+            down_out[...] = whole.reshape(FF, C)
+        elif n == 1:
+            up_out[:, :C] = whole[0].reshape(C, C)
+            up_out[:, C:] = whole[1].reshape(C, C)
+        else:
+            disco_out[(n - 2) * 512 : (n - 1) * 512] = whole.reshape(512, C)
+    for n in range(4):
         gc_copy(n).wait_send()
 
 
-def finish(o, b, g, out_o, out_b, out_disco, out_up, out_down, wdisco, wup, wdown, sem):
-    copies = [
-        pltpu.make_async_copy(o, out_o, sem.at[0]),
-        pltpu.make_async_copy(b, out_b, sem.at[1]),
-        pltpu.make_async_copy(wdisco, out_disco, sem.at[2]),
-        pltpu.make_async_copy(wdown, out_down, sem.at[3]),
-        pltpu.make_async_copy(wup, out_up, sem.at[4]),
-    ]
-    copies[0].start()
-    copies[1].start()
-    wdisco[...] = g[2:].reshape(K * C, C).astype(F32)
-    copies[2].start()
-    wdown[...] = g[0].reshape(FF, C).astype(F32)
-    copies[3].start()
-    wup[:, :C] = g[1, 0].reshape(C, C).astype(F32)
-    wup[:, C:] = g[1, 1].reshape(C, C).astype(F32)
-    copies[4].start()
+def finish(*refs):
+    sem = refs[10]
+    copies = [pltpu.make_async_copy(refs[n], refs[5 + n], sem.at[n]) for n in (2, 3, 4, 0, 1)]
+    for c in copies:
+        c.start()
     for c in copies:
         c.wait()
 
@@ -494,32 +493,30 @@
         vm((4, 4, 4, 16, C), BF16),
         vm((4, 15, 16, C), BF16),
         vm((4, 8, 16, C), BF16),
+        vm((4, 2, 4, 4, 16, C), BF16),
         dma((10,)),
         dma((2, 8)),
         dma((2, 8)),
         dma((4,)),
         dma((4,)),
-        dma((4, 15)),
-        dma((4, 15)),
-        dma((4, 7)),
-        dma((4, 7)),
-        dma((4, 15)),
-        dma((4, 15)),
+        dma((4,)),
+        dma((4,)),
+        dma((4,)),
+        dma((4,)),
+        dma((4,)),
+        dma((4,)),
         dma((4,)),
         dma((4,)),
     ]
+    results = (((TOK, C), BF16), ((TOK, C), BF16), ((K * C, C), F32), ((C, FF), F32), ((FF, C), F32))
     inner = pl.pallas_call(
         kernel,
-        out_shape=(
-            vm((TOK, C), BF16),
-            vm((TOK, C), BF16),
-            vm((4, 2, 4, 4, 16, C), BF16),
-        ),
+        out_shape=[vm(*r) for r in results],
         in_specs=[pl.BlockSpec(memory_space=pltpu.SMEM)] + [pl.BlockSpec(memory_space=pltpu.HBM)] * 10,
-        out_specs=[vspec] * 3,
+        out_specs=[vspec] * 5,
         scratch_shapes=scratch,
         compiler_params=pltpu.CompilerParams(
-            collective_id=0, has_side_effects=True, vmem_limit_bytes=62 * 2**20
+            collective_id=0, has_side_effects=True, vmem_limit_bytes=60 * 2**20
         ),
     )(
         lon_width,
@@ -536,16 +533,10 @@
     )
     out, back, disco, up, down = pl.pallas_call(
         finish,
-        out_shape=(
-            jax.ShapeDtypeStruct((TOK, C), BF16),
-            jax.ShapeDtypeStruct((TOK, C), BF16),
-            jax.ShapeDtypeStruct((K * C, C), F32),
-            jax.ShapeDtypeStruct((C, FF), F32),
-            jax.ShapeDtypeStruct((FF, C), F32),
-        ),
-        in_specs=[vspec] * 3,
+        out_shape=[jax.ShapeDtypeStruct(*r) for r in results],
+        in_specs=[vspec] * 5,
         out_specs=[pl.BlockSpec(memory_space=pltpu.HBM)] * 5,
-        scratch_shapes=[vm((K * C, C), F32), vm((C, FF), F32), vm((FF, C), F32), dma((5,))],
+        scratch_shapes=[dma((5,))],
         compiler_params=pltpu.CompilerParams(vmem_limit_bytes=16 * 2**20),
     )(*[pltpu.with_memory_space_constraint(v, pltpu.VMEM) for v in inner])
     shape = fields.shape

time: 46.6 us -> 43.9 us (0.942)
  Pallas kernels: 45.9 us -> 43.2 us
    pallas_call x2, Pallas kernels: 45.9 us -> 43.2 us  [the longest x1 41.7 us: per_device(): pl.pallas_call(kernel, out_shape=[vm(*r) for r in results], in_specs=[pl....]
where the time goes in v4:
time: 43.9 us; the launch traced here: 43.8 us
  Pallas kernels  43.2 us (98%)
  between operations  0.64 us (1%)
    pallas_call x1, Pallas kernels, per_device(): pl.pallas_call(kernel, out_shape=[vm(*r) for r in results], in_specs=[pl....  41.7 us
    pallas_call x1, Pallas kernels, per_device(): pl.pallas_call(finish, out_shape=[jax.ShapeDtypeStruct(*r) for r in resul...  1.48 us

profile of v4, /device:TPU:1, one launch (start us, length us, event | category | flops | bytes accessed | tf_op | source)
XLA Modules:
  0.0 43.8 jit_solution(3908946206945652872)
XLA Ops:
  0.6 41.7 %shard_map.146 = (bf16[384,256]{1,0:T(8,128)(2,1)S(1)}, bf16[384,256]{1,0:T(8,128)(2,1)S(1)}, f32[1024,256]{1,0:T(8,128)S(1)}, f32[256,512]{1,0:T(8,128)S(1)}, f32[512,256]{1,0:T(8,128)S(1)}) custom-call(s32[64]{0:T(128)} %lw.1, bf16[2,4,48,256]{3,2,1,0:T(8,128)(2,1)} %bitcast.10, bf16[384,256]{1,0:T(8,128)(2,1)} %bitcast.11, bf16[1024,256]{1,0:T(8,128)(2,1)} %bitcast.9, ...), custom_call_target="tpu_custom_call" | custom-call | tf_op jit(solution)/shard_map/pallas_call | solution.py:512
  42.4 1.5 %shard_map.147 = (bf16[384,256]{1,0:T(8,128)(2,1)}, bf16[384,256]{1,0:T(8,128)(2,1)}, f32[1024,256]{1,0:T(8,128)}, f32[256,512]{1,0:T(8,128)}, f32[512,256]{1,0:T(8,128)}) custom-call(bf16[384,256]{1,0:T(8,128)(2,1)S(1)} %get-tuple-element.15.refs_0_, bf16[384,256]{1,0:T(8,128)(2,1)S(1)} %get-tuple-element.16.refs_1_, ...), custom_call_target="tpu_custom_call" | custom-call | tf_op jit(solution)/shard_map/pallas_call | solution.py:534

commit v5 on v4

--- a/solution.py
+++ b/solution.py
@@ -19,8 +19,8 @@
 A_TAPS, B_TAPS = 5, 9
 PAIRS = ROWS // 2
 TOK = M * ROWS * CELLS
-BLOCK = 80
-NK = 3 * BLOCK
+OWN, SIDES = 48, 32
+NK = 3 * (OWN + SIDES)
 NF = A_TAPS * B_TAPS * 8
 PLANE = sorted(
     [(dx, dy) for dx in range(4) for dy in range(4) if dx or dy],
@@ -38,25 +38,29 @@
                 s = (a * B_TAPS + b) * 8 + k
                 sel_f[s, k * 256 + a * 32 + b] = 1
                 sel_b[s, k * 256 + (4 - a) * 32 + 8 - b] = 1
-    perm = np.zeros((2, 256, 256), np.float32)
+    perm = np.zeros((2, 256, M * 256), np.float32)
     for i2 in range(2):
         for a in range(A_TAPS):
             p, r2 = divmod(i2 + a, 2)
             for jj in range(32):
-                if jj < 4:
-                    col = p * BLOCK + 48 + r2 * 4 + jj
-                elif jj < 28:
-                    col = p * BLOCK + r2 * CELLS + jj - 4
-                else:
-                    col = p * BLOCK + 64 + r2 * 4 + jj - 28
-                perm[i2, a * 32 + jj, col] = 1
-    edge = np.zeros((2 * PAIRS * 16, ROWS * CELLS), np.float32)
+                for m in range(M):
+                    side = 3 * OWN + p * SIDES + m * 8 + r2 * 4
+                    if jj < 4:
+                        col = side + jj
+                    elif jj < 28:
+                        col = p * OWN + r2 * CELLS + jj - 4
+                    else:
+                        col = side + 16 + jj - 28
+                    perm[i2, a * 32 + jj, m * 256 + col] = 1
+    edge = np.zeros((2 * PAIRS * 16, TOK), np.float32)
     for side in range(2):
         for q in range(PAIRS):
-            for r2 in range(2):
-                for j in range(4):
-                    cell = (CELLS - 4 + j) if side == 0 else j
-                    edge[(side * PAIRS + q) * 16 + r2 * 4 + j, (q * 2 + r2) * CELLS + cell] = 1
+            for m in range(M):
+                for r2 in range(2):
+                    for j in range(4):
+                        cell = (CELLS - 4 + j) if side == 0 else j
+                        token = ((m * PAIRS + q) * 2 + r2) * CELLS + cell
+                        edge[(side * PAIRS + q) * 16 + m * 8 + r2 * 4 + j, token] = 1
     return [x.astype(jnp.bfloat16) for x in (sel_f, sel_b, perm, edge)]
 
 
@@ -67,7 +71,7 @@
 def kernel(
     lw, fields, cot, disco, up, down, filt, sel_f, sel_b, perm, edge,
     vout, vback, disco_out, up_out, down_out,
-    x, y, stage, vcot, vdisco, vup, vdown, vfilt, filt8, vself, vselb, vperm, vedge,
+    x, y, xs, ys, stage, vcot, vdisco, vup, vdown, vfilt, filt8, vself, vselb, vperm, vedge,
     vline, lines, band, tap_f, tap_b, spread, pre, cd, hidden, bpre, resid, bres,
     g, rc, a1, r1, rz, o,
     lsem, hs, hr, cs, cr, s1s, s1r, zs, zr, g1s, g1r, gcs, gcr,
@@ -89,7 +93,7 @@
     has_up, has_down = lat > 0, lat < 7
 
     loads = [
-        pltpu.make_async_copy(fields, x.at[:, 1:5, 0:48], lsem.at[0]),
+        pltpu.make_async_copy(fields, x.at[:, 1:5], lsem.at[0]),
         pltpu.make_async_copy(edge, vedge, lsem.at[1]),
         pltpu.make_async_copy(filt, vfilt, lsem.at[2]),
         pltpu.make_async_copy(sel_f, vself, lsem.at[3]),
@@ -127,44 +131,45 @@
     for d in RING:
         hello(at_z(d))
 
-    zero48 = jnp.zeros((M, BLOCK, C), BF16)
+    def clear(n):
+        for buf, sides in ((x, xs), (y, ys)):
+            buf[:, n] = jnp.zeros((M, OWN, C), BF16)
+            sides[n] = jnp.zeros((SIDES, C), BF16)
 
     @pl.when(lat == 0)
     def _():
-        x[:, 0] = zero48
-        y[:, 0] = zero48
+        clear(0)
 
     @pl.when(lat == 7)
     def _():
-        x[:, 5] = zero48
-        y[:, 5] = zero48
+        clear(5)
 
     def rdma(src, dst, ss, rs, dev):
         return pltpu.make_async_remote_copy(
             src_ref=src, dst_ref=dst, send_sem=ss, recv_sem=rs, device_id=dev, device_id_type=MESH
         )
 
-    def halo(buf, ph):
+    def halo(buf, sides, ph):
         st = stage.at[ph]
 
         def lon_copies():
             return [
-                rdma(st.at[0], buf.at[:, 1:5, 48:64], hs.at[ph, 0], hr.at[ph, 0], (lat, right)),
-                rdma(st.at[1], buf.at[:, 1:5, 64:80], hs.at[ph, 1], hr.at[ph, 1], (lat, left)),
+                rdma(st.at[0], sides.at[1:5, 0:16], hs.at[ph, 0], hr.at[ph, 0], (lat, right)),
+                rdma(st.at[1], sides.at[1:5, 16:32], hs.at[ph, 1], hr.at[ph, 1], (lat, left)),
             ]
 
         def to_down():
             return [
-                rdma(buf.at[:, 4, 0:48], buf.at[:, 0, 0:48], hs.at[ph, 2], hr.at[ph, 2], (lat + 1, lon)),
-                rdma(st.at[0, :, 3], buf.at[:, 0, 48:64], hs.at[ph, 3], hr.at[ph, 3], (lat + 1, right)),
-                rdma(st.at[1, :, 3], buf.at[:, 0, 64:80], hs.at[ph, 4], hr.at[ph, 4], (lat + 1, left)),
+                rdma(buf.at[:, 4], buf.at[:, 0], hs.at[ph, 2], hr.at[ph, 2], (lat + 1, lon)),
+                rdma(st.at[0, 3], sides.at[0, 0:16], hs.at[ph, 3], hr.at[ph, 3], (lat + 1, right)),
+                rdma(st.at[1, 3], sides.at[0, 16:32], hs.at[ph, 4], hr.at[ph, 4], (lat + 1, left)),
             ]
 
         def to_up():
             return [
-                rdma(buf.at[:, 1, 0:48], buf.at[:, 5, 0:48], hs.at[ph, 5], hr.at[ph, 5], (lat - 1, lon)),
-                rdma(st.at[0, :, 0], buf.at[:, 5, 48:64], hs.at[ph, 6], hr.at[ph, 6], (lat - 1, right)),
-                rdma(st.at[1, :, 0], buf.at[:, 5, 64:80], hs.at[ph, 7], hr.at[ph, 7], (lat - 1, left)),
+                rdma(buf.at[:, 1], buf.at[:, 5], hs.at[ph, 5], hr.at[ph, 5], (lat - 1, lon)),
+                rdma(st.at[0, 0], sides.at[5, 0:16], hs.at[ph, 6], hr.at[ph, 6], (lat - 1, right)),
+                rdma(st.at[1, 0], sides.at[5, 16:32], hs.at[ph, 7], hr.at[ph, 7], (lat - 1, left)),
             ]
 
         def start():
@@ -211,17 +216,15 @@
 
         return start, recv, sent
 
-    halo_x = halo(x, 0)
-    halo_y = halo(y, 1)
+    halo_x = halo(x, xs, 0)
+    halo_y = halo(y, ys, 1)
 
     def own(buf, m):
-        return buf[m, 1:5, 0:48].reshape(ROWS * CELLS, C)
+        return buf[m, 1:5].reshape(ROWS * CELLS, C)
 
     def fill_stage(buf, ph):
-        for m in range(M):
-            e = dot(vedge[...], own(buf, m)).astype(BF16).reshape(2, PAIRS, 16, C)
-            stage[ph, 0, m] = e[0]
-            stage[ph, 1, m] = e[1]
+        e = dot(vedge[...], buf[:, 1:5].reshape(TOK, C)).astype(BF16)
+        stage[ph] = e.reshape(2, PAIRS, 16, C)
 
     loads[0].wait()
     loads[1].wait()
@@ -269,7 +272,8 @@
             for k in range(K):
                 at = q * 96 + k * CELLS
                 both = jnp.concatenate([res[0][at : at + CELLS], res[1][at : at + CELLS]], axis=0)
-                tap[q, k * 48 : (k + 1) * 48] = both.astype(BF16)
+                for m in range(M):
+                    tap[m, q, k * 48 : (k + 1) * 48] = both[:, m * 256 : (m + 1) * 256].astype(BF16)
 
     loads[3].wait()
     loads[4].wait()
@@ -283,16 +287,19 @@
     loads[7].wait()
     loads[8].wait()
 
-    def stencil(tap, buf, dst):
+    def stencil(tap, buf, sides, dst):
         for q in range(PAIRS):
             for m in range(M):
-                res = dot(tap[q][:, :NK], buf[m, q : q + 3].reshape(NK, C)).astype(BF16)
+                window = jnp.concatenate(
+                    [buf[m, q : q + 3].reshape(3 * OWN, C), sides[q : q + 3].reshape(3 * SIDES, C)], axis=0
+                )
+                res = dot(tap[m, q][:, :NK], window).astype(BF16)
                 for k in range(K):
                     at = m * 192 + q * 48
                     dst[at : at + 48, k * C : (k + 1) * C] = res[k * 48 : (k + 1) * 48]
 
     halo_x[1]()
-    stencil(tap_f, x, spread)
+    stencil(tap_f, x, xs, spread)
 
     for m in range(M):
         mixed = dot(spread[m * 192 : (m + 1) * 192], vdisco[...])
@@ -384,7 +391,7 @@
     br = (vcot[...].astype(F32) + dot(bpre[...], vup[...], ((1,), (1,)))).astype(BF16)
     bres[...] = br
     for m in range(M):
-        y[m, 1:5, 0:48] = br[m * 192 : (m + 1) * 192].reshape(PAIRS, 48, C)
+        y[m, 1:5] = br[m * 192 : (m + 1) * 192].reshape(PAIRS, 48, C)
     fill_stage(y, 1)
     do_core(0)
     do_core(1)
@@ -417,7 +424,7 @@
     for n in range(4):
         wait_all(7, zs.at[n])
     halo_y[1]()
-    stencil(tap_b, y, spread)
+    stencil(tap_b, y, ys, spread)
     for m in range(M):
         at = slice(m * 192, (m + 1) * 192)
         acc = bres[at].astype(F32)
@@ -463,9 +470,11 @@
     dma = pltpu.SemaphoreType.DMA
     vm = pltpu.VMEM
     scratch = [
-        vm((M, 6, BLOCK, C), BF16),
-        vm((M, 6, BLOCK, C), BF16),
-        vm((2, 2, M, PAIRS, 16, C), BF16),
+        vm((M, 6, OWN, C), BF16),
+        vm((M, 6, OWN, C), BF16),
+        vm((6, SIDES, C), BF16),
+        vm((6, SIDES, C), BF16),
+        vm((2, 2, PAIRS, 16, C), BF16),
         vm((TOK, C), BF16),
         vm((K * C, C), BF16),
         vm((C, FF), BF16),
@@ -474,13 +483,13 @@
         vm((NF, NLAT), F32),
         vm((NF, K * 256), BF16),
         vm((NF, K * 256), BF16),
-        vm((2, 256, 256), BF16),
-        vm((2 * PAIRS * 16, ROWS * CELLS), BF16),
+        vm((2, 256, M * 256), BF16),
+        vm((2 * PAIRS * 16, TOK), BF16),
         vm((16, K * 256), F32),
         vm((8, K * 256), F32),
         vm((2, PAIRS * 96, 256), BF16),
-        vm((PAIRS, 192, 256), BF16),
-        vm((PAIRS, 192, 256), BF16),
+        vm((M, PAIRS, 192, 256), BF16),
+        vm((M, PAIRS, 192, 256), BF16),
         vm((TOK, K * C), BF16),
         vm((TOK, FF), F32),
         vm((TOK, FF), F32),

time: 43.9 us -> 43.1 us (0.982)
  Pallas kernels: 43.2 us -> 42.4 us
    pallas_call x1, Pallas kernels: 41.7 us -> 40.9 us  [per_device(): pl.pallas_call(kernel, out_shape=[vm(*r) for r in results], in_specs=[pl....]
where the time goes in v5:
time: 43.1 us; the launch traced here: 43 us
  Pallas kernels  42.4 us (98%)
  between operations  0.64 us (1%)
    pallas_call x1, Pallas kernels, per_device(): pl.pallas_call(kernel, out_shape=[vm(*r) for r in results], in_specs=[pl....  40.9 us
    pallas_call x1, Pallas kernels, per_device(): pl.pallas_call(finish, out_shape=[jax.ShapeDtypeStruct(*r) for r in resul...  1.48 us

profile of v5, /device:TPU:1, one launch (start us, length us, event | category | flops | bytes accessed | tf_op | source)
XLA Modules:
  0.0 43.0 jit_solution(13103087563895365199)
XLA Ops:
  0.6 40.9 %shard_map.146 = (bf16[384,256]{1,0:T(8,128)(2,1)S(1)}, bf16[384,256]{1,0:T(8,128)(2,1)S(1)}, f32[1024,256]{1,0:T(8,128)S(1)}, f32[256,512]{1,0:T(8,128)S(1)}, f32[512,256]{1,0:T(8,128)S(1)}) custom-call(s32[64]{0:T(128)} %lw.1, bf16[2,4,48,256]{3,2,1,0:T(8,128)(2,1)} %bitcast.10, bf16[384,256]{1,0:T(8,128)(2,1)} %bitcast.11, bf16[1024,256]{1,0:T(8,128)(2,1)} %bitcast.9, ...), custom_call_target="tpu_custom_call" | custom-call | tf_op jit(solution)/shard_map/pallas_call | solution.py:521
  41.5 1.5 %shard_map.147 = (bf16[384,256]{1,0:T(8,128)(2,1)}, bf16[384,256]{1,0:T(8,128)(2,1)}, f32[1024,256]{1,0:T(8,128)}, f32[256,512]{1,0:T(8,128)}, f32[512,256]{1,0:T(8,128)}) custom-call(bf16[384,256]{1,0:T(8,128)(2,1)S(1)} %get-tuple-element.15.refs_0_, bf16[384,256]{1,0:T(8,128)(2,1)S(1)} %get-tuple-element.16.refs_1_, ...), custom_call_target="tpu_custom_call" | custom-call | tf_op jit(solution)/shard_map/pallas_call | solution.py:543

commit v6 on v5

--- a/solution.py
+++ b/solution.py
@@ -74,7 +74,7 @@
     x, y, xs, ys, stage, vcot, vdisco, vup, vdown, vfilt, filt8, vself, vselb, vperm, vedge,
     vline, lines, band, tap_f, tap_b, spread, pre, cd, hidden, bpre, resid, bres,
     g, rc, a1, r1, rz, o,
-    lsem, hs, hr, cs, cr, s1s, s1r, zs, zr, g1s, g1r, gcs, gcr,
+    lsem, hs, hr, cs, cr, s1s, s1r, zs, zr, g1s, g1r, gcs, gcr, vouch1, vouch2,
 ):
     lat, lon = lax.axis_index("lat"), lax.axis_index("lon")
     x_hi, yy = lat // 4, lat % 4
@@ -125,11 +125,9 @@
         for v in (left, lon, right):
             hello((lat + 1, v))
 
-    hello(pair)
-    for dx, dy in PLANE:
-        hello(at_xy(dx, dy))
-    for d in RING:
-        hello(at_z(d))
+    near_chips = [at_xy(dx, dy) for dx, dy in PLANE if dx != 2 and dy != 2] + [at_z(1), at_z(7)]
+    for dev in near_chips:
+        hello(dev)
 
     def clear(n):
         for buf, sides in ((x, xs), (y, ys)):
@@ -230,9 +228,15 @@
     loads[1].wait()
     fill_stage(x, 0)
     pl.semaphore_wait(
-        barrier, 25 + 3 * has_up.astype(jnp.int32) + 3 * has_down.astype(jnp.int32)
+        barrier, 12 + 3 * has_up.astype(jnp.int32) + 3 * has_down.astype(jnp.int32)
     )
     halo_x[0]()
+
+    def vouch(sem, devs):
+        for dev in devs:
+            pl.semaphore_signal(sem, inc=1, device_id=dev, device_id_type=MESH)
+
+    vouch(vouch1, near_chips)
 
     loads[2].wait()
     filt8[...] = jnp.zeros_like(filt8)
@@ -393,6 +397,8 @@
     for m in range(M):
         y[m, 1:5] = br[m * 192 : (m + 1) * 192].reshape(PAIRS, 48, C)
     fill_stage(y, 1)
+    pl.semaphore_wait(vouch1, 10)
+    vouch(vouch2, [at_z(2), at_z(6)])
     do_core(0)
     do_core(1)
     for n in range(2):
@@ -410,6 +416,7 @@
     lines[...] = total
     bands(lambda i, k: lines[i : i + 1, k * 256 : (k + 1) * 256], tap_b)
 
+    pl.semaphore_wait(vouch2, 2)
     for n in range(4):
         do_plane(n)
 
@@ -516,6 +523,8 @@
         dma((4,)),
         dma((4,)),
         dma((4,)),
+        pltpu.SemaphoreType.REGULAR,
+        pltpu.SemaphoreType.REGULAR,
     ]
     results = (((TOK, C), BF16), ((TOK, C), BF16), ((K * C, C), F32), ((C, FF), F32), ((FF, C), F32))
     inner = pl.pallas_call(

time: 43.1 us -> 42.1 us (0.977)
  Pallas kernels: 42.4 us -> 41.4 us
    pallas_call x1, Pallas kernels: 40.9 us -> 39.9 us  [per_device(): pl.pallas_call(kernel, out_shape=[vm(*r) for r in results], in_specs=[pl....]
where the time goes in v6:
time: 42.1 us; the launch traced here: 42 us
  Pallas kernels  41.4 us (98%)
  between operations  0.64 us (2%)
    pallas_call x1, Pallas kernels, per_device(): pl.pallas_call(kernel, out_shape=[vm(*r) for r in results], in_specs=[pl....  39.9 us
    pallas_call x1, Pallas kernels, per_device(): pl.pallas_call(finish, out_shape=[jax.ShapeDtypeStruct(*r) for r in resul...  1.48 us

profile of v6, /device:TPU:1, one launch (start us, length us, event | category | flops | bytes accessed | tf_op | source)
XLA Modules:
  0.0 42.0 jit_solution(2471274314485246696)
XLA Ops:
  0.6 39.9 %shard_map.146 = (bf16[384,256]{1,0:T(8,128)(2,1)S(1)}, bf16[384,256]{1,0:T(8,128)(2,1)S(1)}, f32[1024,256]{1,0:T(8,128)S(1)}, f32[256,512]{1,0:T(8,128)S(1)}, f32[512,256]{1,0:T(8,128)S(1)}) custom-call(s32[64]{0:T(128)} %lw.1, bf16[2,4,48,256]{3,2,1,0:T(8,128)(2,1)} %bitcast.10, bf16[384,256]{1,0:T(8,128)(2,1)} %bitcast.11, bf16[1024,256]{1,0:T(8,128)(2,1)} %bitcast.9, ...), custom_call_target="tpu_custom_call" | custom-call | tf_op jit(solution)/shard_map/pallas_call | solution.py:530
  40.5 1.5 %shard_map.147 = (bf16[384,256]{1,0:T(8,128)(2,1)}, bf16[384,256]{1,0:T(8,128)(2,1)}, f32[1024,256]{1,0:T(8,128)}, f32[256,512]{1,0:T(8,128)}, f32[512,256]{1,0:T(8,128)}) custom-call(bf16[384,256]{1,0:T(8,128)(2,1)S(1)} %get-tuple-element.15.refs_0_, bf16[384,256]{1,0:T(8,128)(2,1)S(1)} %get-tuple-element.16.refs_1_, ...), custom_call_target="tpu_custom_call" | custom-call | tf_op jit(solution)/shard_map/pallas_call | solution.py:552

commit v7 on v6

--- a/solution.py
+++ b/solution.py
@@ -69,9 +69,9 @@
 
 
 def kernel(
-    lw, fields, cot, disco, up, down, filt, sel_f, sel_b, perm, edge,
+    width, fields, cot, disco, up, down, filt, sel_f, sel_b, perm, edge,
     vout, vback, disco_out, up_out, down_out,
-    x, y, xs, ys, stage, vcot, vdisco, vup, vdown, vfilt, filt8, vself, vselb, vperm, vedge,
+    lw, x, y, xs, ys, stage, vcot, vdisco, vup, vdown, vfilt, filt8, vself, vselb, vperm, vedge,
     vline, lines, band, tap_f, tap_b, spread, pre, cd, hidden, bpre, resid, bres,
     g, rc, a1, r1, rz, o,
     lsem, hs, hr, cs, cr, s1s, s1r, zs, zr, g1s, g1r, gcs, gcr, vouch1, vouch2,
@@ -103,9 +103,10 @@
         pltpu.make_async_copy(disco, vdisco, lsem.at[7]),
         pltpu.make_async_copy(up, vup, lsem.at[8]),
         pltpu.make_async_copy(sel_b, vselb, lsem.at[9]),
+        pltpu.make_async_copy(width, lw, lsem.at[10]),
     ]
-    for c in loads:
-        c.start()
+    loads[0].start()
+    loads[1].start()
 
     barrier = pltpu.get_barrier_semaphore()
 
@@ -128,6 +129,9 @@
     near_chips = [at_xy(dx, dy) for dx, dy in PLANE if dx != 2 and dy != 2] + [at_z(1), at_z(7)]
     for dev in near_chips:
         hello(dev)
+
+    for c in loads[2:]:
+        c.start()
 
     def clear(n):
         for buf, sides in ((x, xs), (y, ys)):
@@ -239,6 +243,7 @@
     vouch(vouch1, near_chips)
 
     loads[2].wait()
+    loads[10].wait()
     filt8[...] = jnp.zeros_like(filt8)
     for n in range(A_TAPS * B_TAPS):
         filt8[n * 8 : n * 8 + K] = vfilt[n].astype(F32)
@@ -477,6 +482,7 @@
     dma = pltpu.SemaphoreType.DMA
     vm = pltpu.VMEM
     scratch = [
+        pltpu.SMEM((NLAT,), jnp.int32),
         vm((M, 6, OWN, C), BF16),
         vm((M, 6, OWN, C), BF16),
         vm((6, SIDES, C), BF16),
@@ -510,7 +516,7 @@
         vm((4, 15, 16, C), BF16),
         vm((4, 8, 16, C), BF16),
         vm((4, 2, 4, 4, 16, C), BF16),
-        dma((10,)),
+        dma((11,)),
         dma((2, 8)),
         dma((2, 8)),
         dma((4,)),
@@ -530,7 +536,7 @@
     inner = pl.pallas_call(
         kernel,
         out_shape=[vm(*r) for r in results],
-        in_specs=[pl.BlockSpec(memory_space=pltpu.SMEM)] + [pl.BlockSpec(memory_space=pltpu.HBM)] * 10,
+        in_specs=[pl.BlockSpec(memory_space=pltpu.HBM)] * 11,
         out_specs=[vspec] * 5,
         scratch_shapes=scratch,
         compiler_params=pltpu.CompilerParams(

time: 42.1 us -> 41.4 us (0.983)
  Pallas kernels: 41.4 us -> 40.7 us
    pallas_call x1, Pallas kernels: 39.9 us -> 39.2 us  [per_device(): pl.pallas_call(kernel, out_shape=[vm(*r) for r in results], in_specs=[pl....]
where the time goes in v7:
time: 41.4 us
  Pallas kernels  40.7 us (98%)
  between operations  0.64 us (2%)
    pallas_call x1, Pallas kernels, per_device(): pl.pallas_call(kernel, out_shape=[vm(*r) for r in results], in_specs=[pl....  39.2 us
    pallas_call x1, Pallas kernels, per_device(): pl.pallas_call(finish, out_shape=[jax.ShapeDtypeStruct(*r) for r in resul...  1.48 us

profile of v7, /device:TPU:1, one launch (start us, length us, event | category | flops | bytes accessed | tf_op | source)
XLA Modules:
  0.0 41.4 jit_solution(17842305206262523790)
XLA Ops:
  0.6 39.2 %shard_map.146 = (bf16[384,256]{1,0:T(8,128)(2,1)S(1)}, bf16[384,256]{1,0:T(8,128)(2,1)S(1)}, f32[1024,256]{1,0:T(8,128)S(1)}, f32[256,512]{1,0:T(8,128)S(1)}, f32[512,256]{1,0:T(8,128)S(1)}) custom-call(s32[64]{0:T(128)} %width.1, bf16[2,4,48,256]{3,2,1,0:T(8,128)(2,1)} %bitcast.10, bf16[384,256]{1,0:T(8,128)(2,1)} %bitcast.11, bf16[1024,256]{1,0:T(8,128)(2,1)} %bitcast.9, ...), custom_call_target="tpu_custom_call" | custom-call | tf_op jit(solution)/shard_map/pallas_call | solution.py:536
  39.9 1.5 %shard_map.147 = (bf16[384,256]{1,0:T(8,128)(2,1)}, bf16[384,256]{1,0:T(8,128)(2,1)}, f32[1024,256]{1,0:T(8,128)}, f32[256,512]{1,0:T(8,128)}, f32[512,256]{1,0:T(8,128)}) custom-call(bf16[384,256]{1,0:T(8,128)(2,1)S(1)} %get-tuple-element.15.refs_0_, bf16[384,256]{1,0:T(8,128)(2,1)S(1)} %get-tuple-element.16.refs_1_, ...), custom_call_target="tpu_custom_call" | custom-call | tf_op jit(solution)/shard_map/pallas_call | solution.py:558

commit v8 on v7

--- a/solution.py
+++ b/solution.py
@@ -22,10 +22,7 @@
 OWN, SIDES = 48, 32
 NK = 3 * (OWN + SIDES)
 NF = A_TAPS * B_TAPS * 8
-PLANE = sorted(
-    [(dx, dy) for dx in range(4) for dy in range(4) if dx or dy],
-    key=lambda t: (-min(t[0], 4 - t[0]) - min(t[1], 4 - t[1]), t),
-)
+PLANE = [(2, 2), (2, 1), (1, 2), (2, 3), (3, 2), (1, 1), (3, 3), (1, 3), (3, 1), (2, 0), (0, 2), (1, 0), (0, 1), (3, 0), (0, 3)]
 RING = (4, 3, 5, 2, 6, 1, 7)
 
 

time: 41.4 us -> 41.5 us (level)
  no operation moved by 1% of the time
where the time goes in v8:
time: 41.5 us
  Pallas kernels  40.8 us (98%)
  between operations  0.64 us (2%)
    pallas_call x1, Pallas kernels, per_device(): pl.pallas_call(kernel, out_shape=[vm(*r) for r in results], in_specs=[pl....  39.3 us
    pallas_call x1, Pallas kernels, per_device(): pl.pallas_call(finish, out_shape=[jax.ShapeDtypeStruct(*r) for r in resul...  1.48 us

profile of v8, /device:TPU:1, one launch (start us, length us, event | category | flops | bytes accessed | tf_op | source)
XLA Modules:
  0.0 41.5 jit_solution(6974918690406498982)
XLA Ops:
  0.6 39.3 %shard_map.146 = (bf16[384,256]{1,0:T(8,128)(2,1)S(1)}, bf16[384,256]{1,0:T(8,128)(2,1)S(1)}, f32[1024,256]{1,0:T(8,128)S(1)}, f32[256,512]{1,0:T(8,128)S(1)}, f32[512,256]{1,0:T(8,128)S(1)}) custom-call(s32[64]{0:T(128)} %width.1, bf16[2,4,48,256]{3,2,1,0:T(8,128)(2,1)} %bitcast.10, bf16[384,256]{1,0:T(8,128)(2,1)} %bitcast.11, bf16[1024,256]{1,0:T(8,128)(2,1)} %bitcast.9, ...), custom_call_target="tpu_custom_call" | custom-call | tf_op jit(solution)/shard_map/pallas_call | solution.py:533
  40.0 1.5 %shard_map.147 = (bf16[384,256]{1,0:T(8,128)(2,1)}, bf16[384,256]{1,0:T(8,128)(2,1)}, f32[1024,256]{1,0:T(8,128)}, f32[256,512]{1,0:T(8,128)}, f32[512,256]{1,0:T(8,128)}) custom-call(bf16[384,256]{1,0:T(8,128)(2,1)S(1)} %get-tuple-element.15.refs_0_, bf16[384,256]{1,0:T(8,128)(2,1)S(1)} %get-tuple-element.16.refs_1_, ...), custom_call_target="tpu_custom_call" | custom-call | tf_op jit(solution)/shard_map/pallas_call | solution.py:555
